TPU v7x, 32 devices: a whole 2x2x4 slice. The times are simulated.
32 devices in a mesh: aperture: 16 (over z, y, core), range: 2 (over x).
Axes of the slice: x: 2, y: 2, z: 4, core: 2. Of those that a mesh axis runs over, the one named last changes fastest.
Arguments:
- echoes: bfloat16 [2, 512, 8192], P(None, 'aperture', 'range'), may hold values from -6 to 6
- transmit_chirp: bfloat16 [2, 512], replicated, may hold values from -0.1875 to 0.1875
- band_weights: float32 [4, 2, 2, 512, 16], P(None, None, None, 'aperture'), may hold values from -0.75 to 0.75
- band_offsets: int32 [4, 2, 512], P(None, None, 'aperture'), may hold values from -16 to 16
- band_widths: int32 [4, 2, 512], P(None, None, 'aperture'), may hold values from 8 to 16
- child_rows: int32 [4, 512], P(None, 'aperture'), may hold values from 0 to 15
Outputs:
- subimage: bfloat16 [2, 512, 8192], P(None, 'aperture', 'range')
All inputs are finite; a program needn't handle non-finite values.
Results may differ from a plain program's by a relative error of at most 0.007.
Values may be sent and summed in bfloat16 or wider, within the bound.
A program may use at most 128 MiB of HBM per device.

v0:
```python
import jax
import jax.numpy as jnp
from jax import lax
from jax.sharding import PartitionSpec as P

KERN = 16
SHIFT = 16
LEVELS = 4


def partner(block, axis, stride):
    count = lax.axis_size(axis)
    route = []
    for low in range(count):
        high = low | 1 << stride
        if high != low and high < count:
            route += [(low, high), (high, low)]
    return lax.ppermute(block, axis, route)


def with_halo(cells, sides, width):
    for axis, dim in sides:
        count = lax.axis_size(axis)
        ends = count - 1
        head = lax.slice_in_dim(cells, 0, width, axis=dim)
        tail = lax.slice_in_dim(cells, cells.shape[dim] - width, cells.shape[dim], axis=dim)
        cells = jnp.concatenate(
            [
                lax.ppermute(tail, axis, [(i, (i + 1) % count) for i in range(ends)]),
                cells,
                lax.ppermute(head, axis, [((i + 1) % count, i) for i in range(ends)]),
            ],
            axis=dim,
        )
    return cells


def compress(padded, transmit_chirp, out_length):
    chirp_real = transmit_chirp[0]
    chirp_imag = transmit_chirp[1]
    kernel = jnp.stack([jnp.stack([chirp_real, chirp_imag]), jnp.stack([-chirp_imag, chirp_real])])
    result = lax.conv_general_dilated(
        padded,
        kernel,
        (1,),
        "VALID",
        dimension_numbers=("CNW", "OIW", "CNW"),
        preferred_element_type=jnp.float32,
    )
    return result[:, :, :out_length]


def shifted_sum(source, kernel, offsets_now, widths_now, child_index, margin, out_length):
    kern_taps = kernel.shape[-1]
    half_count = source.shape[1]
    span = 2 * SHIFT + kern_taps
    base = margin - kern_taps // 2 - SHIFT
    picker = (child_index[:, None] == jnp.arange(half_count, dtype=jnp.int32)[None, :]).astype(
        source.dtype
    )
    rows_in = jnp.einsum("pc,scr->spr", picker, source, preferred_element_type=jnp.float32).astype(
        jnp.bfloat16
    )
    live_taps = (jnp.arange(kern_taps, dtype=jnp.int32)[None, :] < widths_now[:, None]).astype(
        jnp.float32
    )
    weights = kernel * live_taps[None]
    tap_shift = (
        jnp.arange(span, dtype=jnp.int32)[:, None] - jnp.arange(kern_taps, dtype=jnp.int32)[None, :]
    )
    placed = (tap_shift[None, :, :] == (offsets_now + SHIFT)[:, None, None]).astype(jnp.float32)
    spread = jnp.sum(weights[:, :, None, :] * placed[None], axis=3)
    real_part = jnp.zeros((rows_in.shape[1], out_length), jnp.float32)
    imag_part = jnp.zeros((rows_in.shape[1], out_length), jnp.float32)
    for tap_index in range(span):
        shifted = rows_in[:, :, base + tap_index : base + tap_index + out_length].astype(
            jnp.float32
        )
        weight_real = spread[0, :, tap_index : tap_index + 1]
        weight_imag = spread[1, :, tap_index : tap_index + 1]
        real_part = real_part + weight_real * shifted[0] - weight_imag * shifted[1]
        imag_part = imag_part + weight_real * shifted[1] + weight_imag * shifted[0]
    return jnp.stack([real_part, imag_part])


def merge_rows(
    lower_child, upper_child, kernel, offsets_now, widths_now, child_index, margin, out_length
):
    lower_term = shifted_sum(
        lower_child, kernel[0], offsets_now[0], widths_now[0], child_index, margin, out_length
    )
    upper_term = shifted_sum(
        upper_child, kernel[1], offsets_now[1], widths_now[1], child_index, margin, out_length
    )
    return lower_term + upper_term


def trade(half_block, level_index):
    return partner(half_block, "aperture", level_index)


def body(echoes, transmit_chirp, band_weights, band_offsets, band_widths, child_rows):
    pulse_rows = echoes.shape[1]
    half_rows = pulse_rows // 2
    range_bins = echoes.shape[2]
    tap_count = transmit_chirp.shape[1]
    margin = SHIFT + KERN // 2
    padded = with_halo(echoes, (("range", 2),), tap_count // 2)
    subimage = compress(padded, transmit_chirp, range_bins).astype(jnp.bfloat16)
    position = lax.axis_index("range") * range_bins
    total_bins = range_bins * lax.axis_size("range")
    for level_index in range(LEVELS):
        subimage = with_halo(subimage, (("range", 2),), margin)
        side_bit = lax.axis_index("aperture") >> level_index & 1
        kept_half = lax.dynamic_slice_in_dim(subimage, side_bit * half_rows, half_rows, 1)
        sent_half = lax.dynamic_slice_in_dim(subimage, (1 - side_bit) * half_rows, half_rows, 1)
        received = trade(sent_half, level_index)
        lower_child = jnp.where(side_bit == 0, kept_half, received)
        upper_child = jnp.where(side_bit == 0, received, kept_half)
        out_length = subimage.shape[2] - 2 * margin
        merged = merge_rows(
            lower_child,
            upper_child,
            band_weights[level_index],
            band_offsets[level_index],
            band_widths[level_index],
            child_rows[level_index],
            margin,
            out_length,
        )
        rim_width = (out_length - range_bins) // 2
        global_bins = position - rim_width + jnp.arange(out_length, dtype=jnp.int32)
        inside = (global_bins >= 0) & (global_bins < total_bins)
        subimage = jnp.where(inside, merged, 0.0).astype(jnp.bfloat16)
    return subimage


def solution(mesh):
    return jax.shard_map(
        body,
        mesh=mesh,
        in_specs=(
            P(None, "aperture", "range"),
            P(),
            P(None, None, None, "aperture", None),
            P(None, None, "aperture"),
            P(None, None, "aperture"),
            P(None, "aperture"),
        ),
        out_specs=P(None, "aperture", "range"),
        check_vma=False,
    )
```

profile of v0, /device:TPU:0, one launch (start us, length us, event | category | flops | bytes accessed | tf_op | source)
XLA Modules:
  0.0 871.3 jit_solution(17299091079789873551)
XLA Ops:
  54.7 402.3 %convolution_convert_fusion.8 = bf16[2,32,4096]{1,0,2:T(2,128)(2,1)S(1)} fusion(bf16[2,32,4608]{1,0,2:T(2,128)(2,1)S(1)} %copy.68, bf16[2,2,512]{1,0,2:T(2,128)(2,1)S(1)} %copy.69), kind=kOutput, calls=%fused_computation.16 | convolution fusion | flops 537133056 | bytes 1118208 | tf_op jit(solution)/shard_map/slice | solution.py:50
  488.1 13.4 %multiply_subtract_fusion.6 = f32[1,32,4096]{2,1,0:T(8,128)} fusion(f32[2,32,4096]{2,1,0:T(8,128)S(1)} %get-tuple-element.1056, f32[2,32,4096]{2,1,0:T(8,128)S(1)} %get-tuple-element.1057, f32[2,32,4096]{2,1,0:T(8,128)S(1)} %get-tuple-element.1058, f32[2,32,4096]{2,1,0:T(8,128)S(1)} %get-tuple-element.1059, f32[2,32,4096]{2,1,0:T(8,128)S(1)} %get-tuple-element.1060, ...), kind=kLoop, calls=%fused_computation.430 | loop fusion | flops 25034752 | bytes 50868224 | tf_op jit(solution)/shard_map/sub | solution.py:81
  501.7 11.6 %multiply_add_fusion.6 = f32[1,32,4096]{2,1,0:T(8,128)} fusion(f32[2,32,4096]{2,1,0:T(8,128)S(1)} %get-tuple-element.1056, f32[2,32,4096]{2,1,0:T(8,128)S(1)} %get-tuple-element.1057, f32[2,32,4096]{2,1,0:T(8,128)S(1)} %get-tuple-element.1058, f32[2,32,4096]{2,1,0:T(8,128)S(1)} %get-tuple-element.1059, f32[2,32,4096]{2,1,0:T(8,128)S(1)} %get-tuple-element.1060, ...), kind=kLoop, calls=%fused_computation.429 | loop fusion | flops 25034752 | bytes 50868224 | tf_op jit(solution)/shard_map/add | solution.py:82
  518.0 7.4 slice_convert_fusion.382
  531.6 13.2 %multiply_subtract_fusion.7 = f32[1,32,4096]{2,1,0:T(8,128)} fusion(f32[2,32,4096]{2,1,0:T(8,128)S(1)} %get-tuple-element.1104, f32[2,32,4096]{2,1,0:T(8,128)S(1)} %get-tuple-element.1105, f32[2,32,4096]{2,1,0:T(8,128)S(1)} %get-tuple-element.1106, f32[2,32,4096]{2,1,0:T(8,128)S(1)} %get-tuple-element.1107, f32[2,32,4096]{2,1,0:T(8,128)S(1)} %get-tuple-element.1108, ...), kind=kLoop, calls=%fused_computation.433 | loop fusion | flops 25034752 | bytes 50868224 | tf_op jit(solution)/shard_map/sub | solution.py:81
  544.9 11.8 %multiply_add_fusion.7 = f32[1,32,4096]{2,1,0:T(8,128)} fusion(f32[2,32,4096]{2,1,0:T(8,128)S(1)} %get-tuple-element.1104, f32[2,32,4096]{2,1,0:T(8,128)S(1)} %get-tuple-element.1105, f32[2,32,4096]{2,1,0:T(8,128)S(1)} %get-tuple-element.1106, f32[2,32,4096]{2,1,0:T(8,128)S(1)} %get-tuple-element.1107, f32[2,32,4096]{2,1,0:T(8,128)S(1)} %get-tuple-element.1108, ...), kind=kLoop, calls=%fused_computation.432 | loop fusion | flops 25034752 | bytes 50868224 | tf_op jit(solution)/shard_map/add | solution.py:82
  580.3 7.4 slice_convert_fusion.238
  593.6 13.1 %multiply_subtract_fusion.4 = f32[1,32,4096]{2,1,0:T(8,128)} fusion(f32[2,32,4096]{2,1,0:T(8,128)S(1)} %get-tuple-element.960, f32[2,32,4096]{2,1,0:T(8,128)S(1)} %get-tuple-element.961, f32[2,32,4096]{2,1,0:T(8,128)S(1)} %get-tuple-element.962, f32[2,32,4096]{2,1,0:T(8,128)S(1)} %get-tuple-element.963, f32[2,32,4096]{2,1,0:T(8,128)S(1)} %get-tuple-element.964, ...), kind=kLoop, calls=%fused_computation.425 | loop fusion | flops 25034752 | bytes 50868224 | tf_op jit(solution)/shard_map/sub | solution.py:81
  607.0 11.6 %multiply_add_fusion.4 = f32[1,32,4096]{2,1,0:T(8,128)} fusion(f32[2,32,4096]{2,1,0:T(8,128)S(1)} %get-tuple-element.960, f32[2,32,4096]{2,1,0:T(8,128)S(1)} %get-tuple-element.961, f32[2,32,4096]{2,1,0:T(8,128)S(1)} %get-tuple-element.962, f32[2,32,4096]{2,1,0:T(8,128)S(1)} %get-tuple-element.963, f32[2,32,4096]{2,1,0:T(8,128)S(1)} %get-tuple-element.964, ...), kind=kLoop, calls=%fused_computation.424 | loop fusion | flops 25034752 | bytes 50868224 | tf_op jit(solution)/shard_map/add | solution.py:82
  622.9 7.4 slice_convert_fusion.286
  636.4 13.1 %multiply_subtract_fusion.5 = f32[1,32,4096]{2,1,0:T(8,128)} fusion(f32[2,32,4096]{2,1,0:T(8,128)S(1)} %get-tuple-element.1008, f32[2,32,4096]{2,1,0:T(8,128)S(1)} %get-tuple-element.1009, f32[2,32,4096]{2,1,0:T(8,128)S(1)} %get-tuple-element.1010, f32[2,32,4096]{2,1,0:T(8,128)S(1)} %get-tuple-element.1011, f32[2,32,4096]{2,1,0:T(8,128)S(1)} %get-tuple-element.1012, ...), kind=kLoop, calls=%fused_computation.428 | loop fusion | flops 25034752 | bytes 50868224 | tf_op jit(solution)/shard_map/sub | solution.py:81
  649.8 11.9 %multiply_add_fusion.5 = f32[1,32,4096]{2,1,0:T(8,128)} fusion(f32[2,32,4096]{2,1,0:T(8,128)S(1)} %get-tuple-element.1008, f32[2,32,4096]{2,1,0:T(8,128)S(1)} %get-tuple-element.1009, f32[2,32,4096]{2,1,0:T(8,128)S(1)} %get-tuple-element.1010, f32[2,32,4096]{2,1,0:T(8,128)S(1)} %get-tuple-element.1011, f32[2,32,4096]{2,1,0:T(8,128)S(1)} %get-tuple-element.1012, ...), kind=kLoop, calls=%fused_computation.427 | loop fusion | flops 25034752 | bytes 50868224 | tf_op jit(solution)/shard_map/add | solution.py:82
  682.1 7.4 slice_convert_fusion.142
  695.5 13.1 %multiply_subtract_fusion.2 = f32[1,32,4096]{2,1,0:T(8,128)} fusion(f32[2,32,4096]{2,1,0:T(8,128)S(1)} %get-tuple-element.864, f32[2,32,4096]{2,1,0:T(8,128)S(1)} %get-tuple-element.865, f32[2,32,4096]{2,1,0:T(8,128)S(1)} %get-tuple-element.866, f32[2,32,4096]{2,1,0:T(8,128)S(1)} %get-tuple-element.867, f32[2,32,4096]{2,1,0:T(8,128)S(1)} %get-tuple-element.868, ...), kind=kLoop, calls=%fused_computation.420 | loop fusion | flops 25034752 | bytes 50868224 | tf_op jit(solution)/shard_map/sub | solution.py:81
  708.9 11.6 %multiply_add_fusion.2 = f32[1,32,4096]{2,1,0:T(8,128)} fusion(f32[2,32,4096]{2,1,0:T(8,128)S(1)} %get-tuple-element.864, f32[2,32,4096]{2,1,0:T(8,128)S(1)} %get-tuple-element.865, f32[2,32,4096]{2,1,0:T(8,128)S(1)} %get-tuple-element.866, f32[2,32,4096]{2,1,0:T(8,128)S(1)} %get-tuple-element.867, f32[2,32,4096]{2,1,0:T(8,128)S(1)} %get-tuple-element.868, ...), kind=kLoop, calls=%fused_computation.419 | loop fusion | flops 25034752 | bytes 50868224 | tf_op jit(solution)/shard_map/add | solution.py:82
  724.8 7.4 slice_convert_fusion.190
  738.3 13.1 %multiply_subtract_fusion.3 = f32[1,32,4096]{2,1,0:T(8,128)} fusion(f32[2,32,4096]{2,1,0:T(8,128)S(1)} %get-tuple-element.912, f32[2,32,4096]{2,1,0:T(8,128)S(1)} %get-tuple-element.913, f32[2,32,4096]{2,1,0:T(8,128)S(1)} %get-tuple-element.914, f32[2,32,4096]{2,1,0:T(8,128)S(1)} %get-tuple-element.915, f32[2,32,4096]{2,1,0:T(8,128)S(1)} %get-tuple-element.916, ...), kind=kLoop, calls=%fused_computation.423 | loop fusion | flops 25034752 | bytes 50868224 | tf_op jit(solution)/shard_map/sub | solution.py:81
  751.7 11.9 %multiply_add_fusion.3 = f32[1,32,4096]{2,1,0:T(8,128)} fusion(f32[2,32,4096]{2,1,0:T(8,128)S(1)} %get-tuple-element.912, f32[2,32,4096]{2,1,0:T(8,128)S(1)} %get-tuple-element.913, f32[2,32,4096]{2,1,0:T(8,128)S(1)} %get-tuple-element.914, f32[2,32,4096]{2,1,0:T(8,128)S(1)} %get-tuple-element.915, f32[2,32,4096]{2,1,0:T(8,128)S(1)} %get-tuple-element.916, ...), kind=kLoop, calls=%fused_computation.422 | loop fusion | flops 25034752 | bytes 50868224 | tf_op jit(solution)/shard_map/add | solution.py:82
  787.3 7.4 slice_convert_fusion.46
  800.7 13.1 %multiply_subtract_fusion = f32[1,32,4096]{2,1,0:T(8,128)} fusion(f32[2,32,4096]{2,1,0:T(8,128)S(1)} %get-tuple-element.768, f32[2,32,4096]{2,1,0:T(8,128)S(1)} %get-tuple-element.769, f32[2,32,4096]{2,1,0:T(8,128)S(1)} %get-tuple-element.770, f32[2,32,4096]{2,1,0:T(8,128)S(1)} %get-tuple-element.771, f32[2,32,4096]{2,1,0:T(8,128)S(1)} %get-tuple-element.772, ...), kind=kLoop, calls=%fused_computation.415 | loop fusion | flops 25034752 | bytes 50868224 | tf_op jit(solution)/shard_map/sub | solution.py:81
  814.1 11.6 %multiply_add_fusion = f32[1,32,4096]{2,1,0:T(8,128)} fusion(f32[2,32,4096]{2,1,0:T(8,128)S(1)} %get-tuple-element.768, f32[2,32,4096]{2,1,0:T(8,128)S(1)} %get-tuple-element.769, f32[2,32,4096]{2,1,0:T(8,128)S(1)} %get-tuple-element.770, f32[2,32,4096]{2,1,0:T(8,128)S(1)} %get-tuple-element.771, f32[2,32,4096]{2,1,0:T(8,128)S(1)} %get-tuple-element.772, ...), kind=kLoop, calls=%fused_computation.414 | loop fusion | flops 25034752 | bytes 50868224 | tf_op jit(solution)/shard_map/add | solution.py:82
  830.1 7.4 slice_convert_fusion.94
  843.7 13.1 %multiply_subtract_fusion.1 = f32[1,32,4096]{2,1,0:T(8,128)} fusion(f32[2,32,4096]{2,1,0:T(8,128)S(1)} %get-tuple-element.816, f32[2,32,4096]{2,1,0:T(8,128)S(1)} %get-tuple-element.817, f32[2,32,4096]{2,1,0:T(8,128)S(1)} %get-tuple-element.818, f32[2,32,4096]{2,1,0:T(8,128)S(1)} %get-tuple-element.819, f32[2,32,4096]{2,1,0:T(8,128)S(1)} %get-tuple-element.820, ...), kind=kLoop, calls=%fused_computation.418 | loop fusion | flops 25034752 | bytes 50868224 | tf_op jit(solution)/shard_map/sub | solution.py:81
  857.0 11.7 %multiply_add_fusion.1 = f32[1,32,4096]{2,1,0:T(8,128)} fusion(f32[2,32,4096]{2,1,0:T(8,128)S(1)} %get-tuple-element.816, f32[2,32,4096]{2,1,0:T(8,128)S(1)} %get-tuple-element.817, f32[2,32,4096]{2,1,0:T(8,128)S(1)} %get-tuple-element.818, f32[2,32,4096]{2,1,0:T(8,128)S(1)} %get-tuple-element.819, f32[2,32,4096]{2,1,0:T(8,128)S(1)} %get-tuple-element.820, ...), kind=kLoop, calls=%fused_computation.417 | loop fusion | flops 25034752 | bytes 50868224 | tf_op jit(solution)/shard_map/add | solution.py:82
  (858 shorter events, 212.1 us)
Async XLA Ops:
  0.8 50.8 %collective-permute-start = (bf16[2,32,256]{2,1,0:T(8,128)(2,1)S(1)}, bf16[2,32,256]{2,1,0:T(8,128)(2,1)S(1)}, u32[]{:S(2)}, u32[]{:S(2)}) collective-permute-start(bf16[2,32,256]{2,1,0:T(8,128)(2,1)S(1)} %get-tuple-element.1157), channel_id=1, source_target_pairs={{0,1},{2,3},{4,5},{6,7},{8,9},{10,11},{12,13},{14,15},{16,17},{18,... | collective-permute-start | bytes 98312 | tf_op jit(solution)/shard_map/ppermute | solution.py:29
  5.6 46.0 %collective-permute-start.1 = (bf16[2,32,256]{2,1,0:T(8,128)(2,1)S(1)}, bf16[2,32,256]{2,1,0:T(8,128)(2,1)S(1)}, u32[]{:S(2)}, u32[]{:S(2)}) collective-permute-start(bf16[2,32,256]{2,1,0:T(8,128)(2,1)S(1)} %get-tuple-element.1158), channel_id=1, source_target_pairs={{1,0},{3,2},{5,4},{7,6},{9,8},{11,10},{13,12},{15,14},{17,16},{19,... | collective-permute-start | bytes 98312 | tf_op jit(solution)/shard_map/ppermute | solution.py:31
  54.7 408.4 %copy-start.13 = (f32[2,32,48]{2,1,0:T(8,128)S(1)}, f32[2,32,48]{2,1,0:T(8,128)}, u32[]{:S(2)}) copy-start(f32[2,32,48]{2,1,0:T(8,128)} %copy-done.12) | copy-start | bytes 36868
  457.0 11.4 %collective-permute-start.2 = (bf16[2,32,24]{1,0,2:T(2,128)(2,1)S(1)}, bf16[2,32,24]{1,0,2:T(2,128)(2,1)S(1)}, u32[]{:S(2)}, u32[]{:S(2)}) collective-permute-start(bf16[2,32,24]{1,0,2:T(2,128)(2,1)S(1)} %get-tuple-element.766), channel_id=1, source_target_pairs={{0,1},{2,3},{4,5},{6,7},{8,9},{10,11},{12,13},{14,15},{16,17},{18,... | collective-permute-start | bytes 9224 | tf_op jit(solution)/shard_map/ppermute | solution.py:29
  461.6 7.0 collective-permute-start.3
  469.3 1.6 collective-permute-start.4
  487.9 13.6 %copy-start.14 = (f32[2,32,4096]{2,1,0:T(8,128)S(1)}, f32[2,32,4096]{2,1,0:T(8,128)}, u32[]{:S(2)}) copy-start(f32[2,32,4096]{2,1,0:T(8,128)} %get-tuple-element.1077) | copy-start | bytes 3145732
  487.9 13.6 %copy-start.15 = (f32[2,32,4096]{2,1,0:T(8,128)S(1)}, f32[2,32,4096]{2,1,0:T(8,128)}, u32[]{:S(2)}) copy-start(f32[2,32,4096]{2,1,0:T(8,128)} %get-tuple-element.1078) | copy-start | bytes 3145732
  487.9 13.6 %copy-start.16 = (f32[2,32,4096]{2,1,0:T(8,128)S(1)}, f32[2,32,4096]{2,1,0:T(8,128)}, u32[]{:S(2)}) copy-start(f32[2,32,4096]{2,1,0:T(8,128)} %get-tuple-element.1079) | copy-start | bytes 3145732
  487.9 13.6 %copy-start.17 = (f32[2,32,4096]{2,1,0:T(8,128)S(1)}, f32[2,32,4096]{2,1,0:T(8,128)}, u32[]{:S(2)}) copy-start(f32[2,32,4096]{2,1,0:T(8,128)} %get-tuple-element.1080) | copy-start | bytes 3145732
  487.9 13.6 %copy-start.18 = (f32[2,32,4096]{2,1,0:T(8,128)S(1)}, f32[2,32,4096]{2,1,0:T(8,128)}, u32[]{:S(2)}) copy-start(f32[2,32,4096]{2,1,0:T(8,128)} %get-tuple-element.1081) | copy-start | bytes 3145732
  558.1 14.7 %copy-start = (f32[2,32,48]{2,1,0:T(8,128)S(1)}, f32[2,32,48]{2,1,0:T(8,128)}, u32[]{:S(2)}) copy-start(f32[2,32,48]{2,1,0:T(8,128)} %get-tuple-element.1198) | copy-start | bytes 36868
  558.2 18.3 %copy-start.349 = (s32[32]{0:T(128)S(1)}, s32[32]{0:T(128)}, u32[]{:S(2)}) copy-start(s32[32]{0:T(128)} %get-tuple-element.1192) | copy-start | bytes 388
  558.2 6.7 collective-permute-start.5
  562.8 5.6 collective-permute-start.6
  569.3 7.2 collective-permute-start.7
  663.1 15.3 %copy-start.348 = (s32[32]{0:T(128)S(1)}, s32[32]{0:T(128)}, u32[]{:S(2)}) copy-start(s32[32]{0:T(128)} %get-tuple-element.1194) | copy-start | bytes 388
  663.1 4.1 collective-permute-start.8
  665.2 5.6 collective-permute-start.9
  671.9 6.5 collective-permute-start.10
  765.0 18.6 %copy-start.347 = (s32[32]{0:T(128)S(1)}, s32[32]{0:T(128)}, u32[]{:S(2)}) copy-start(s32[32]{0:T(128)} %get-tuple-element.1191) | copy-start | bytes 388
  765.0 3.8 collective-permute-start.11
  766.8 5.6 collective-permute-start.12
  773.3 10.3 %collective-permute-start.13 = (bf16[2,16,4144]{2,1,0:T(8,128)(2,1)S(1)}, bf16[2,16,4144]{2,1,0:T(8,128)(2,1)S(1)}, u32[]{:S(2)}, u32[]{:S(2)}) collective-permute-start(bf16[2,16,4144]{2,1,0:T(8,128)(2,1)S(1)} %constant_dynamic-slice_fusion), channel_id=1, source_target_pairs={{0,16},{16,0},{2,18},{18,2},{4,20},{20,4},{6,22},{22,6},{8,24},{24... | collective-permute-start | bytes 795656 | tf_op jit(solution)/shard_map/ppermute | solution.py:18
  (342 other events, 3551.9 us)
where the time goes:
time: 881 us; the launch traced here: 871 us
  matrix products  408 us (46%)
  other arithmetic  338 us (38%)
  local copies, waits for them, and re-layouts  67.5 us (8%)
  starting transfers between devices  30.5 us (3%)
  waiting for transfers between devices  20.9 us (2%)
    slice x1, matrix products, compress(): return result[:, :, :out_length]  402 us
    convert_element_type x24, other arithmetic, shifted_sum(): rows_in[:, :, base + tap_index:base + tap_index + out_length]  129 us
    sub x8, other arithmetic, shifted_sum(): real_part = real_part + weight_real * shifted[0] - weight_imag * shifted[1]  105 us
    add x8, other arithmetic, shifted_sum(): imag_part = imag_part + weight_real * shifted[1] + weight_imag * shifted[0]  93.7 us
    slice x24, local copies, waits for them, and re-layouts, shifted_sum(): weight_real = spread[0, :, tap_index:tap_index + 1]  26.6 us
    slice x24, local copies, waits for them, and re-layouts, shifted_sum(): weight_imag = spread[1, :, tap_index:tap_index + 1]  23.7 us
    ppermute x5, starting transfers between devices, with_halo(): lax.ppermute(tail, axis, [(i, (i + 1) % count) for i in range(ends)])  17.8 us
  transfers between devices with their start and end apart: 14, of which 7 were waited for; matrix products, arithmetic and copies ran while one was open for 7% of the time, Pallas kernels for 0%

commit v1 on v0

v1 whole, which is shorter than its diff:
```python
import functools

import jax
import jax.numpy as jnp
from jax import lax
from jax.experimental import pallas as pl
from jax.experimental.pallas import tpu as pltpu
from jax.sharding import PartitionSpec as P

KERN = 16
SHIFT = 16
LEVELS = 4
PH = 4
MARGIN = SHIFT + KERN // 2
REACH = MARGIN // PH
STEPS = 2 * REACH + 1
RIM = LEVELS * MARGIN
BLOCK = 256
HALF = 16
PARAMS = pltpu.CompilerParams(vmem_limit_bytes=48 * 1024 * 1024)


def partner(block, axis, stride):
    count = lax.axis_size(axis)
    route = []
    for low in range(count):
        high = low | 1 << stride
        if high != low and high < count:
            route += [(low, high), (high, low)]
    return lax.ppermute(block, axis, route)


def with_halo(cells, axis, dim, width):
    count = lax.axis_size(axis)
    ends = count - 1
    head = lax.slice_in_dim(cells, 0, width, axis=dim)
    tail = lax.slice_in_dim(cells, cells.shape[dim] - width, cells.shape[dim], axis=dim)
    return jnp.concatenate(
        [
            lax.ppermute(tail, axis, [(i, (i + 1) % count) for i in range(ends)]),
            cells,
            lax.ppermute(head, axis, [((i + 1) % count, i) for i in range(ends)]),
        ],
        axis=dim,
    )


def split_store(y, scal_ref, kept_ref, sent_ref):
    row = lax.broadcasted_iota(jnp.int32, y.shape, 0) + scal_ref[0]
    y = jnp.where((row >= 0) & (row < scal_ref[1]), y, 0.0)
    first = y[:, :128]
    second = y[:, 128:]
    upper = scal_ref[2] == 1
    kept_ref[...] = jnp.where(upper, second, first).astype(jnp.bfloat16)
    sent_ref[...] = jnp.where(upper, first, second).astype(jnp.bfloat16)


def compress_kernel(blocks, window, scal_ref, e_ref, t_ref, kept_ref, sent_ref, y_ref):
    rows = BLOCK // PH
    for b in range(blocks):
        w = e_ref[b * BLOCK : b * BLOCK + window, :]
        acc = jnp.dot(t_ref[0], w[:, :64], preferred_element_type=jnp.float32)
        acc = acc + jnp.dot(t_ref[1], w[:, 64:], preferred_element_type=jnp.float32)
        parts = [
            acc[po * rows : (po + 1) * rows, hb * 32 : hb * 32 + 32]
            for hb in range(2)
            for po in range(PH)
        ]
        y_ref[b * rows : (b + 1) * rows, :] = jnp.concatenate(parts, axis=1)
    split_store(y_ref[...], scal_ref, kept_ref, sent_ref)


def merge_kernel(last, out_rows, *refs):
    scal_ref, kept_in, recv_in, wl_ref, off_ref, child_ref = refs[:6]
    if last:
        perm_ref, out_ref, x_ref, y_ref, g_ref, hi_ref, lo_ref = refs[6:]
    else:
        kept_ref, sent_ref, x_ref, y_ref, g_ref, hi_ref, lo_ref = refs[6:]
    rows = kept_in.shape[0]
    x_ref[0:8, :] = jnp.zeros((8, 256), jnp.float32)
    x_ref[rows + 8 : rows + 16, :] = jnp.zeros((8, 256), jnp.float32)
    x_ref[8 : rows + 8, :128] = kept_in[...].astype(jnp.float32)
    x_ref[8 : rows + 8, 128:] = recv_in[...].astype(jnp.float32)
    span = 56
    u = lax.broadcasted_iota(jnp.int32, (span, 256), 0)
    for t in range(2):
        tap = u - MARGIN + KERN // 2 - off_ref[t : t + 1, :]
        for ri in range(2):
            g = jnp.zeros((span, 256), jnp.float32)
            for k in range(KERN):
                g = jnp.where(tap == k, wl_ref[2 * t + ri, k : k + 1, :], g)
            high = g.astype(jnp.bfloat16).astype(jnp.float32)
            g_ref[2 * t + ri] = high
            g_ref[4 + 2 * t + ri] = g - high
    mine = lax.broadcasted_iota(jnp.int32, (HALF, 256), 0) == child_ref[0:1, :]
    for q in range(STEPS):
        for t in range(2):
            for pi in range(PH):
                for ri in range(2):
                    r0 = t * 128 + pi * 32 + ri * 16
                    s = q * PH + pi
                    high = g_ref[2 * t + ri, s : s + 1, :]
                    low = g_ref[4 + 2 * t + ri, s : s + 1, :]
                    hi_ref[q, r0 : r0 + 16, :] = jnp.where(mine, high, 0.0).astype(jnp.bfloat16)
                    lo_ref[q, r0 : r0 + 16, :] = jnp.where(mine, low, 0.0).astype(jnp.bfloat16)
    tile = rows // 2
    for m in range(2):
        acc = jnp.zeros((tile, 256), jnp.float32)
        for q in range(STEPS):
            start = m * tile + 8 - REACH + q
            x = x_ref[start : start + tile, :].astype(jnp.bfloat16)
            acc = acc + jnp.dot(x, hi_ref[q], preferred_element_type=jnp.float32)
            acc = acc + jnp.dot(x, lo_ref[q], preferred_element_type=jnp.float32)
        y_ref[m * tile : (m + 1) * tile, :] = acc
    if not last:
        split_store(y_ref[...], scal_ref, kept_ref, sent_ref)
        return
    for chunk in range(out_rows // 128):
        base = RIM // PH + chunk * 128
        yt = y_ref[base : base + 128, :].T
        for hb in range(2):
            acc = jnp.zeros((32, PH * 128), jnp.float32)
            for po in range(PH):
                r0 = hb * 128 + po * 32
                acc = acc + jnp.dot(
                    yt[r0 : r0 + 32].astype(jnp.bfloat16),
                    perm_ref[po],
                    preferred_element_type=jnp.float32,
                )
            acc = acc.astype(jnp.bfloat16)
            lanes = slice(chunk * PH * 128, (chunk + 1) * PH * 128)
            for ro in range(2):
                out_ref[ro, hb * 16 : hb * 16 + 16, lanes] = acc[ro * 16 : ro * 16 + 16]


def body(echoes, transmit_chirp, band_weights, band_offsets, band_widths, child_rows):
    range_bins = echoes.shape[2]
    taps = transmit_chirp.shape[1]
    halo = taps // 2 + RIM
    blocks = -(-(range_bins + 2 * RIM) // BLOCK)
    rows = blocks * (BLOCK // PH)
    window = BLOCK + taps
    length = blocks * BLOCK + taps
    ap = lax.axis_index("aperture")
    first_row = lax.axis_index("range") * (range_bins // PH) - RIM // PH
    total_rows = range_bins * lax.axis_size("range") // PH

    vm = pl.BlockSpec(memory_space=pltpu.VMEM)
    sm = pl.BlockSpec(memory_space=pltpu.SMEM)
    half_shape = jax.ShapeDtypeStruct((rows, 128), jnp.bfloat16)

    def scalars(level):
        bit = ap >> level & 1
        return jnp.stack([first_row, jnp.int32(total_rows), bit]).astype(jnp.int32)

    padded = with_halo(echoes, "range", 2, halo)
    padded = jnp.pad(padded, ((0, 0), (0, 0), (0, length - padded.shape[2])))
    turned = jnp.stack([padded[1], -padded[0]])
    both = jnp.stack([padded, turned]).reshape(2, 2, 2, HALF, length)
    e_t = both.transpose(0, 2, 1, 3, 4).reshape(128, length).T

    ring = jnp.pad(transmit_chirp, ((0, 0), (0, window + 1 - taps)))
    toep = jnp.tile(ring, (1, BLOCK))[:, : BLOCK * window].reshape(2, BLOCK // PH, PH, window)
    toep = toep.transpose(0, 2, 1, 3).reshape(2, BLOCK, window)

    kept, sent = pl.pallas_call(
        functools.partial(compress_kernel, blocks, window),
        out_shape=(half_shape, half_shape),
        in_specs=[sm, vm, vm],
        out_specs=(vm, vm),
        scratch_shapes=[pltpu.VMEM((rows, 256), jnp.float32)],
        compiler_params=PARAMS,
        name="compress",
    )(scalars(0), e_t, toep)

    side = jnp.stack([ap >> level & 1 for level in range(LEVELS)])
    live = jnp.arange(KERN, dtype=jnp.int32) < band_widths[..., None]
    w = jnp.where(live[:, :, None], band_weights, 0.0)
    w = jnp.where(side[:, None, None, None, None] == 0, w, w[:, ::-1])
    w = w.transpose(0, 1, 2, 4, 3).reshape(LEVELS, 2, 2, KERN, 2, 1, 1, HALF)
    wr, wi = w[:, :, 0], w[:, :, 1]
    wl = jnp.stack(
        [jnp.concatenate([wr, wi], axis=5), jnp.concatenate([-wi, wr], axis=5)], axis=2
    )
    wl = jnp.broadcast_to(wl, (LEVELS, 2, 2, KERN, 2, PH, 2, HALF)).reshape(LEVELS, 4, KERN, 256)
    off = jnp.where(side[:, None, None] == 0, band_offsets, band_offsets[:, ::-1])
    off = off.reshape(LEVELS, 2, 2, 1, 1, HALF) + jnp.arange(PH, dtype=jnp.int32)[:, None, None]
    off = jnp.broadcast_to(off, (LEVELS, 2, 2, PH, 2, HALF)).reshape(LEVELS, 2, 256)
    child = child_rows.reshape(LEVELS, 1, 2, 1, 1, HALF)
    child = jnp.broadcast_to(child, (LEVELS, 1, 2, PH, 2, HALF)).reshape(LEVELS, 1, 256)
    bins = jnp.arange(PH * 128, dtype=jnp.int32)
    perm = (
        bins[None, None, :]
        == PH * jnp.arange(128, dtype=jnp.int32)[None, :, None]
        + jnp.arange(PH, dtype=jnp.int32)[:, None, None]
    ).astype(jnp.bfloat16)

    for level in range(LEVELS):
        received = partner(sent, "aperture", level)
        last = level == LEVELS - 1
        operands = [scalars(level + 1), kept, received, wl[level], off[level], child[level]]
        if last:
            operands.append(perm)
        result = pl.pallas_call(
            functools.partial(merge_kernel, last, range_bins // PH),
            out_shape=jax.ShapeDtypeStruct(echoes.shape, jnp.bfloat16)
            if last
            else (half_shape, half_shape),
            in_specs=[sm] + [vm] * (len(operands) - 1),
            out_specs=vm if last else (vm, vm),
            scratch_shapes=[
                pltpu.VMEM((rows + 16, 256), jnp.float32),
                pltpu.VMEM((rows, 256), jnp.float32),
                pltpu.VMEM((8, 56, 256), jnp.float32),
                pltpu.VMEM((STEPS, 256, 256), jnp.bfloat16),
                pltpu.VMEM((STEPS, 256, 256), jnp.bfloat16),
            ],
            compiler_params=PARAMS,
            name="merge_last" if last else "merge",
        )(*operands)
        if last:
            return result
        kept, sent = result


def solution(mesh):
    return jax.shard_map(
        body,
        mesh=mesh,
        in_specs=(
            P(None, "aperture", "range"),
            P(),
            P(None, None, None, "aperture", None),
            P(None, None, "aperture"),
            P(None, None, "aperture"),
            P(None, "aperture"),
        ),
        out_specs=P(None, "aperture", "range"),
        check_vma=False,
    )
```

time: 881 us -> 80 us (0.09); the launches traced: 871 us -> 79.2 us
  matrix products: 408 us -> 0 us
  other arithmetic: 338 us -> 3.3 us
  local copies, waits for them, and re-layouts: 67.5 us -> 16.1 us
  Pallas kernels: 0 us -> 25.1 us
  starting transfers between devices: 30.5 us -> 12.7 us
    slice x1 -> x0, matrix products: 402 us -> none  [compress(): return result[:, :, :out_length]]
    convert_element_type x37 -> x1, other arithmetic: 135 us -> 0.16 us  [body(): perm = (bins[None, None, :] == PH * jnp.arange(128, dtype=jnp.int32)[None...]
    sub x9 -> x0, other arithmetic: 105 us -> none  [the longest x8 105 us: shifted_sum(): real_part = real_part + weight_real * shifted[0] - weight_imag * shifted[1]]
    add x9 -> x2, other arithmetic: 94.5 us -> 0.01 us  [the longest x1 0.01 us: body(): off.reshape(LEVELS, 2, 2, 1, 1, HALF)]
    slice x49 -> x11, local copies, waits for them, and re-layouts: 51.1 us -> 1.96 us  [the longest x1 0.61 us: body(): off[level]]
    pallas_call x0 -> x5, Pallas kernels: none -> 25.1 us  [the longest x4 20.7 us: body(): pl.pallas_call(functools.partial(merge_kernel, last, range_bins // PH), o...]
    ppermute x5 -> x1, starting transfers between devices: 17.8 us -> 5.45 us  [with_halo(): lax.ppermute(tail, axis, [(i, (i + 1) % count) for i in range(ends)])]
    ppermute x4, waiting for transfers between devices: 10.2 us -> 21.6 us  [partner(): return lax.ppermute(block, axis, route)]
  transfers between devices with their start and end apart: 14 -> 6, of which waited for: 7 -> 3; matrix products, arithmetic and copies ran while one was open for 7% -> 16% of each run, Pallas kernels for 0% -> 0%
where the time goes in v1:
time: 80 us; the launch traced here: 79.2 us
  Pallas kernels  25.1 us (31%)
  waiting for transfers between devices  21.7 us (27%)
  local copies, waits for them, and re-layouts  16.1 us (20%)
  starting transfers between devices  12.7 us (16%)
  other arithmetic  3.3 us (4%)
    ppermute x4, waiting for transfers between devices, partner(): return lax.ppermute(block, axis, route)  21.6 us
    pallas_call x4, Pallas kernels, body(): pl.pallas_call(functools.partial(merge_kernel, last, range_bins // PH), o...  20.7 us
    ppermute x4, starting transfers between devices, partner(): return lax.ppermute(block, axis, route)  5.95 us
    ppermute x1, starting transfers between devices, with_halo(): lax.ppermute(tail, axis, [(i, (i + 1) % count) for i in range(ends)])  5.45 us
    pallas_call x1, Pallas kernels, body(): pl.pallas_call(functools.partial(compress_kernel, blocks, window), out_sh...  4.41 us
    broadcast_in_dim x8, local copies, waits for them, and re-layouts, body(): jnp.broadcast_to(wl, (LEVELS, 2, 2, KERN, 2, PH, 2, HALF))  3.45 us
    another operation x2, local copies, waits for them, and re-layouts, body(): jnp.tile(ring, (1, BLOCK))[:, :BLOCK * window]  2.46 us
    reshape x1, local copies, waits for them, and re-layouts, body(): e_t = both.transpose(0, 2, 1, 3, 4).reshape(128, length).T  2.03 us
  transfers between devices with their start and end apart: 6, of which 3 were waited for; matrix products, arithmetic and copies ran while one was open for 16% of the time, Pallas kernels for 0%

profile of v1, /device:TPU:0, one launch (start us, length us, event | category | flops | bytes accessed | tf_op | source)
XLA Modules:
  0.0 79.2 jit_solution(13589338280131295209)
XLA Ops:
  0.0 1.5 %fusion.10 = (bf16[2,32,352]{2,1,0:T(8,128)(2,1)}, bf16[2,32,352]{2,1,0:T(8,128)(2,1)}) fusion(bf16[2,32,4096]{2,1,0:T(8,128)(2,1)} %param.6), kind=kLoop, calls=%fused_computation.48 | loop fusion | bytes 180224 | tf_op jit(solution)/shard_map/slice | solution.py:36
  1.5 5.4 %collective-permute-start = (bf16[2,32,352]{2,1,0:T(8,128)(2,1)}, bf16[2,32,352]{2,1,0:T(8,128)(2,1)}, u32[]{:S(2)}, u32[]{:S(2)}) collective-permute-start(bf16[2,32,352]{2,1,0:T(8,128)(2,1)} %get-tuple-element.32), channel_id=1, source_target_pairs={{0,1},{2,3},{4,5},{6,7},{8,9},{10,11},{12,13},{14,15},{16,17},{18,... | collective-permute-start | bytes 135176 | tf_op jit(solution)/shard_map/ppermute | solution.py:40
  7.0 1.3 %collective-permute-start.1 = (bf16[2,32,352]{2,1,0:T(8,128)(2,1)}, bf16[2,32,352]{2,1,0:T(8,128)(2,1)}, u32[]{:S(2)}, u32[]{:S(2)}) collective-permute-start(bf16[2,32,352]{2,1,0:T(8,128)(2,1)} %get-tuple-element.31), channel_id=1, source_target_pairs={{1,0},{3,2},{5,4},{7,6},{9,8},{11,10},{13,12},{15,14},{17,16},{19,... | collective-permute-start | bytes 135176 | tf_op jit(solution)/shard_map/ppermute | solution.py:42
  8.3 0.7 iota_compare_fusion.1
  9.0 0.9 %broadcast_select_fusion = f32[4,2,2,32,16]{3,4,2,1,0:T(8,128)S(1)} fusion(f32[4,2,2,32,16]{3,4,2,1,0:T(8,128)} %param.8, pred[4,2,32,16]{2,3,1,0:T(8,128)(4,1)S(1)} %iota_compare_fusion.1), kind=kLoop, calls=%fused_computation.25 | loop fusion | flops 8192 | bytes 69632 | tf_op jit(solution)/shard_map/jit(_where)/select_n | solution.py:178
  11.7 2.4 %tile.10 = bf16[2,196864]{1,0:T(2,128)(2,1)S(1)} reshape(bf16[2,256,769]{2,1,0:T(8,128)(2,1)S(1)} %tile.4) | data formatting | bytes 1574912 | tf_op jit(solution)/shard_map/tile | solution.py:163
  15.7 1.3 %concatenate.18 = bf16[2,32,4800]{2,1,0:T(8,128)(2,1)S(1)} concatenate(bf16[2,32,352]{2,1,0:T(8,128)(2,1)} %collective-permute-done, bf16[2,32,4096]{2,1,0:T(8,128)(2,1)S(1)} %copy-done, bf16[2,32,352]{2,1,0:T(8,128)(2,1)} %collective-permute-done.1), dimensions={2} | concatenate | bytes 1228800 | tf_op jit(solution)/shard_map/concatenate | solution.py:38
  17.4 1.1 %copy.21 = bf16[2,2,2,16,4864]{4,3,2,1,0:T(8,128)(2,1)} copy(bf16[2,2,2,16,4864]{4,3,1,2,0:T(8,128)(2,1)S(1)} %maximum_bitcast_fusion) | data formatting | bytes 2490368 | tf_op jit(solution)/shard_map/transpose | solution.py:160
  18.5 2.0 %copy.22 = bf16[128,4864]{0,1:T(8,128)(2,1)S(1)} copy(bf16[128,4864]{1,0:T(8,128)(2,1)} %bitcast.48) | data formatting | bytes 2490368 | tf_op jit(solution)/shard_map/reshape | solution.py:160
  20.5 4.4 %compress.1 = (bf16[1088,128]{1,0:T(8,128)(2,1)S(1)}, bf16[1088,128]{1,0:T(8,128)(2,1)S(1)}) custom-call(s32[3]{0:T(128)S(1)} %pad_add_fusion.5.scal_ref, bf16[4864,128]{1,0:T(8,128)(2,1)S(1)} %bitcast.46, bf16[2,256,768]{2,1,0:T(8,128)(2,1)S(1)} %bitcast.47), custom_call_target="tpu_custom_call" | custom-call | tf_op jit(solution)/shard_map/compress/pallas_call | solution.py:166
  25.6 0.7 broadcast_in_dim.97.refs_3_
  26.7 4.6 %merge.3 = (bf16[1088,128]{1,0:T(8,128)(2,1)S(1)}, bf16[1088,128]{1,0:T(8,128)(2,1)S(1)}) custom-call(s32[3]{0:T(128)S(1)} %pad_add_fusion.4.refs_0_, bf16[1088,128]{1,0:T(8,128)(2,1)S(1)} %get-tuple-element.13.refs_1_, bf16[1088,128]{1,0:T(8,128)(2,1)S(1)} %collective-permute-done.2.refs_2_, f32[4,16,256]{2,1,0:T(8,128)S(1)} %broadcast_in_dim.97.refs_3_, ...), custom_call_target="tpu_custom_call" | custom-call | tf_op jit(solution)/shard_map/merge/pallas_call | solution.py:204
  31.4 1.6 %collective-permute-start.3 = (bf16[1088,128]{1,0:T(8,128)(2,1)S(1)}, bf16[1088,128]{1,0:T(8,128)(2,1)S(1)}, u32[]{:S(2)}, u32[]{:S(2)}) collective-permute-start(bf16[1088,128]{1,0:T(8,128)(2,1)S(1)} %get-tuple-element.16), channel_id=1, source_target_pairs={{0,4},{4,0},{2,6},{6,2},{8,12},{12,8},{10,14},{14,10},{16,20},{20,... | collective-permute-start | bytes 835592 | tf_op jit(solution)/shard_map/ppermute | solution.py:30
  33.2 0.7 broadcast_in_dim.104.refs_3_
  34.4 6.1 %collective-permute-done.3.refs_2_ = bf16[1088,128]{1,0:T(8,128)(2,1)S(1)} collective-permute-done((bf16[1088,128]{1,0:T(8,128)(2,1)S(1)}, bf16[1088,128]{1,0:T(8,128)(2,1)S(1)}, u32[]{:S(2)}, u32[]{:S(2)}) %collective-permute-start.3) | collective-permute-done | bytes 278560 | tf_op jit(solution)/shard_map/ppermute | solution.py:30
  40.5 4.9 %merge.4 = (bf16[1088,128]{1,0:T(8,128)(2,1)S(1)}, bf16[1088,128]{1,0:T(8,128)(2,1)S(1)}) custom-call(s32[3]{0:T(128)S(1)} %pad_add_fusion.3.refs_0_, bf16[1088,128]{1,0:T(8,128)(2,1)S(1)} %get-tuple-element.15.refs_1_, bf16[1088,128]{1,0:T(8,128)(2,1)S(1)} %collective-permute-done.3.refs_2_, f32[4,16,256]{2,1,0:T(8,128)S(1)} %broadcast_in_dim.104.refs_3_, ...), custom_call_target="tpu_custom_call" | custom-call | tf_op jit(solution)/shard_map/merge/pallas_call | solution.py:204
  45.4 1.6 %collective-permute-start.4 = (bf16[1088,128]{1,0:T(8,128)(2,1)S(1)}, bf16[1088,128]{1,0:T(8,128)(2,1)S(1)}, u32[]{:S(2)}, u32[]{:S(2)}) collective-permute-start(bf16[1088,128]{1,0:T(8,128)(2,1)S(1)} %get-tuple-element.18), channel_id=1, source_target_pairs={{0,8},{8,0},{2,10},{10,2},{4,12},{12,4},{6,14},{14,6},{16,24},{24,... | collective-permute-start | bytes 835592 | tf_op jit(solution)/shard_map/ppermute | solution.py:30
  47.3 0.7 broadcast_in_dim.110.refs_3_
  48.3 5.4 %collective-permute-done.4.refs_2_ = bf16[1088,128]{1,0:T(8,128)(2,1)S(1)} collective-permute-done((bf16[1088,128]{1,0:T(8,128)(2,1)S(1)}, bf16[1088,128]{1,0:T(8,128)(2,1)S(1)}, u32[]{:S(2)}, u32[]{:S(2)}) %collective-permute-start.4) | collective-permute-done | bytes 278560 | tf_op jit(solution)/shard_map/ppermute | solution.py:30
  53.7 4.6 %merge.5 = (bf16[1088,128]{1,0:T(8,128)(2,1)S(1)}, bf16[1088,128]{1,0:T(8,128)(2,1)S(1)}) custom-call(s32[3]{0:T(128)S(1)} %pad_add_fusion.2.refs_0_, bf16[1088,128]{1,0:T(8,128)(2,1)S(1)} %get-tuple-element.17.refs_1_, bf16[1088,128]{1,0:T(8,128)(2,1)S(1)} %collective-permute-done.4.refs_2_, f32[4,16,256]{2,1,0:T(8,128)S(1)} %broadcast_in_dim.110.refs_3_, ...), custom_call_target="tpu_custom_call" | custom-call | tf_op jit(solution)/shard_map/merge/pallas_call | solution.py:204
  58.3 2.6 %collective-permute-start.5 = (bf16[1088,128]{1,0:T(8,128)(2,1)S(1)}, bf16[1088,128]{1,0:T(8,128)(2,1)S(1)}, u32[]{:S(2)}, u32[]{:S(2)}) collective-permute-start(bf16[1088,128]{1,0:T(8,128)(2,1)S(1)} %get-tuple-element.20), channel_id=1, source_target_pairs={{0,16},{16,0},{2,18},{18,2},{4,20},{20,4},{6,22},{22,6},{8,24},{24... | collective-permute-start | bytes 835592 | tf_op jit(solution)/shard_map/ppermute | solution.py:30
  61.3 0.7 broadcast_in_dim.116.refs_3_
  62.5 10.1 %collective-permute-done.5.refs_2_ = bf16[1088,128]{1,0:T(8,128)(2,1)S(1)} collective-permute-done((bf16[1088,128]{1,0:T(8,128)(2,1)S(1)}, bf16[1088,128]{1,0:T(8,128)(2,1)S(1)}, u32[]{:S(2)}, u32[]{:S(2)}) %collective-permute-start.5) | collective-permute-done | bytes 278560 | tf_op jit(solution)/shard_map/ppermute | solution.py:30
  72.6 6.6 %merge_last.1 = bf16[2,32,4096]{2,1,0:T(8,128)(2,1)} custom-call(s32[3]{0:T(128)S(1)} %pad_add_fusion.refs_0_, bf16[1088,128]{1,0:T(8,128)(2,1)S(1)} %get-tuple-element.19.refs_1_, bf16[1088,128]{1,0:T(8,128)(2,1)S(1)} %collective-permute-done.5.refs_2_, f32[4,16,256]{2,1,0:T(8,128)S(1)} %broadcast_in_dim.116.refs_3_, ...), custom_call_target="tpu_custom_call" | custom-call | tf_op jit(solution)/shard_map/merge_last/pallas_call | solution.py:204
  (76 shorter events, 6.5 us)
Async XLA Ops:
  0.0 10.4 %copy-start.4 = (s32[4,2,32]{2,1,0:T(2,128)S(1)}, s32[4,2,32]{2,1,0:T(2,128)}, u32[]{:S(2)}) copy-start(s32[4,2,32]{2,1,0:T(2,128)} %param.9) | copy-start | bytes 3076
  1.5 13.8 %collective-permute-start = (bf16[2,32,352]{2,1,0:T(8,128)(2,1)}, bf16[2,32,352]{2,1,0:T(8,128)(2,1)}, u32[]{:S(2)}, u32[]{:S(2)}) collective-permute-start(bf16[2,32,352]{2,1,0:T(8,128)(2,1)} %get-tuple-element.32), channel_id=1, source_target_pairs={{0,1},{2,3},{4,5},{6,7},{8,9},{10,11},{12,13},{14,15},{16,17},{18,... | collective-permute-start | bytes 135176 | tf_op jit(solution)/shard_map/ppermute | solution.py:40
  7.0 8.3 %collective-permute-start.1 = (bf16[2,32,352]{2,1,0:T(8,128)(2,1)}, bf16[2,32,352]{2,1,0:T(8,128)(2,1)}, u32[]{:S(2)}, u32[]{:S(2)}) collective-permute-start(bf16[2,32,352]{2,1,0:T(8,128)(2,1)} %get-tuple-element.31), channel_id=1, source_target_pairs={{1,0},{3,2},{5,4},{7,6},{9,8},{11,10},{13,12},{15,14},{17,16},{19,... | collective-permute-start | bytes 135176 | tf_op jit(solution)/shard_map/ppermute | solution.py:42
  10.0 1.6 %copy-start.5 = (bf16[2,512]{1,0:T(2,128)(2,1)S(1)}, bf16[2,512]{1,0:T(2,128)(2,1)}, u32[]{:S(2)}) copy-start(bf16[2,512]{1,0:T(2,128)(2,1)} %param.7) | copy-start | bytes 6148
  14.7 1.0 %copy-start = (bf16[2,32,4096]{2,1,0:T(8,128)(2,1)S(1)}, bf16[2,32,4096]{2,1,0:T(8,128)(2,1)}, u32[]{:S(2)}) copy-start(bf16[2,32,4096]{2,1,0:T(8,128)(2,1)} %param.6) | copy-start | bytes 1572868
  25.0 1.8 %collective-permute-start.2 = (bf16[1088,128]{1,0:T(8,128)(2,1)S(1)}, bf16[1088,128]{1,0:T(8,128)(2,1)S(1)}, u32[]{:S(2)}, u32[]{:S(2)}) collective-permute-start(bf16[1088,128]{1,0:T(8,128)(2,1)S(1)} %get-tuple-element.14), channel_id=1, source_target_pairs={{0,2},{2,0},{4,6},{6,4},{8,10},{10,8},{12,14},{14,12},{16,18},{18,... | collective-permute-start | bytes 835592 | tf_op jit(solution)/shard_map/ppermute | solution.py:30
  25.0 1.3 %copy-start.3 = (s32[2,2,4,16]{3,2,1,0:T(4,128)S(1)}, s32[2,2,4,16]{3,2,1,0:T(4,128)}, u32[]{:S(2)}) copy-start(s32[2,2,4,16]{3,2,1,0:T(4,128)} %get-tuple-element.40) | copy-start | bytes 3076
  25.1 1.4 %copy-start.6 = (s32[4,32]{1,0:T(4,128)S(1)}, s32[4,32]{1,0:T(4,128)}, u32[]{:S(2)}) copy-start(s32[4,32]{1,0:T(4,128)} %param.11) | copy-start | bytes 1540
  26.3 7.6 %copy-start.2 = (s32[2,2,4,16]{3,2,1,0:T(4,128)S(1)}, s32[2,2,4,16]{3,2,1,0:T(4,128)}, u32[]{:S(2)}) copy-start(s32[2,2,4,16]{3,2,1,0:T(4,128)} %get-tuple-element.39) | copy-start | bytes 3076
  31.4 9.1 %collective-permute-start.3 = (bf16[1088,128]{1,0:T(8,128)(2,1)S(1)}, bf16[1088,128]{1,0:T(8,128)(2,1)S(1)}, u32[]{:S(2)}, u32[]{:S(2)}) collective-permute-start(bf16[1088,128]{1,0:T(8,128)(2,1)S(1)} %get-tuple-element.16), channel_id=1, source_target_pairs={{0,4},{4,0},{2,6},{6,2},{8,12},{12,8},{10,14},{14,10},{16,20},{20,... | collective-permute-start | bytes 835592 | tf_op jit(solution)/shard_map/ppermute | solution.py:30
  33.9 14.0 %copy-start.1 = (s32[2,2,4,16]{3,2,1,0:T(4,128)S(1)}, s32[2,2,4,16]{3,2,1,0:T(4,128)}, u32[]{:S(2)}) copy-start(s32[2,2,4,16]{3,2,1,0:T(4,128)} %get-tuple-element.38) | copy-start | bytes 3076
  45.4 8.3 %collective-permute-start.4 = (bf16[1088,128]{1,0:T(8,128)(2,1)S(1)}, bf16[1088,128]{1,0:T(8,128)(2,1)S(1)}, u32[]{:S(2)}, u32[]{:S(2)}) collective-permute-start(bf16[1088,128]{1,0:T(8,128)(2,1)S(1)} %get-tuple-element.18), channel_id=1, source_target_pairs={{0,8},{8,0},{2,10},{10,2},{4,12},{12,4},{6,14},{14,6},{16,24},{24,... | collective-permute-start | bytes 835592 | tf_op jit(solution)/shard_map/ppermute | solution.py:30
  58.3 14.3 %collective-permute-start.5 = (bf16[1088,128]{1,0:T(8,128)(2,1)S(1)}, bf16[1088,128]{1,0:T(8,128)(2,1)S(1)}, u32[]{:S(2)}, u32[]{:S(2)}) collective-permute-start(bf16[1088,128]{1,0:T(8,128)(2,1)S(1)} %get-tuple-element.20), channel_id=1, source_target_pairs={{0,16},{16,0},{2,18},{18,2},{4,20},{20,4},{6,22},{22,6},{8,24},{24... | collective-permute-start | bytes 835592 | tf_op jit(solution)/shard_map/ppermute | solution.py:30

commit v2 on v1

--- a/solution.py
+++ b/solution.py
@@ -16,6 +16,7 @@
 STEPS = 2 * REACH + 1
 RIM = LEVELS * MARGIN
 BLOCK = 256
+PIECES = 2
 HALF = 16
 PARAMS = pltpu.CompilerParams(vmem_limit_bytes=48 * 1024 * 1024)
 
@@ -55,10 +56,10 @@
     sent_ref[...] = jnp.where(upper, first, second).astype(jnp.bfloat16)
 
 
-def compress_kernel(blocks, window, scal_ref, e_ref, t_ref, kept_ref, sent_ref, y_ref):
+def compress_kernel(start, blocks, window, scal_ref, e_ref, t_ref, kept_ref, sent_ref, y_ref):
     rows = BLOCK // PH
     for b in range(blocks):
-        w = e_ref[b * BLOCK : b * BLOCK + window, :]
+        w = e_ref[(start + b) * BLOCK : (start + b) * BLOCK + window, :]
         acc = jnp.dot(t_ref[0], w[:, :64], preferred_element_type=jnp.float32)
         acc = acc + jnp.dot(t_ref[1], w[:, 64:], preferred_element_type=jnp.float32)
         parts = [
@@ -67,7 +68,7 @@
             for po in range(PH)
         ]
         y_ref[b * rows : (b + 1) * rows, :] = jnp.concatenate(parts, axis=1)
-    split_store(y_ref[...], scal_ref, kept_ref, sent_ref)
+    split_store(y_ref[: kept_ref.shape[0], :], scal_ref, kept_ref, sent_ref)
 
 
 def merge_kernel(last, out_rows, *refs):
@@ -103,15 +104,13 @@
                     low = g_ref[4 + 2 * t + ri, s : s + 1, :]
                     hi_ref[q, r0 : r0 + 16, :] = jnp.where(mine, high, 0.0).astype(jnp.bfloat16)
                     lo_ref[q, r0 : r0 + 16, :] = jnp.where(mine, low, 0.0).astype(jnp.bfloat16)
-    tile = rows // 2
-    for m in range(2):
-        acc = jnp.zeros((tile, 256), jnp.float32)
-        for q in range(STEPS):
-            start = m * tile + 8 - REACH + q
-            x = x_ref[start : start + tile, :].astype(jnp.bfloat16)
-            acc = acc + jnp.dot(x, hi_ref[q], preferred_element_type=jnp.float32)
-            acc = acc + jnp.dot(x, lo_ref[q], preferred_element_type=jnp.float32)
-        y_ref[m * tile : (m + 1) * tile, :] = acc
+    acc = jnp.zeros((rows, 256), jnp.float32)
+    for q in range(STEPS):
+        start = 8 - REACH + q
+        x = x_ref[start : start + rows, :].astype(jnp.bfloat16)
+        acc = acc + jnp.dot(x, hi_ref[q], preferred_element_type=jnp.float32)
+        acc = acc + jnp.dot(x, lo_ref[q], preferred_element_type=jnp.float32)
+    y_ref[...] = acc
     if not last:
         split_store(y_ref[...], scal_ref, kept_ref, sent_ref)
         return
@@ -137,10 +136,11 @@
     range_bins = echoes.shape[2]
     taps = transmit_chirp.shape[1]
     halo = taps // 2 + RIM
-    blocks = -(-(range_bins + 2 * RIM) // BLOCK)
-    rows = blocks * (BLOCK // PH)
+    piece_bins = range_bins // PIECES
+    blocks = -(-(piece_bins + 2 * RIM) // BLOCK)
+    rows = (piece_bins + 2 * RIM) // PH
     window = BLOCK + taps
-    length = blocks * BLOCK + taps
+    length = (PIECES - 1) * piece_bins + blocks * BLOCK + taps
     ap = lax.axis_index("aperture")
     first_row = lax.axis_index("range") * (range_bins // PH) - RIM // PH
     total_rows = range_bins * lax.axis_size("range") // PH
@@ -149,9 +149,10 @@
     sm = pl.BlockSpec(memory_space=pltpu.SMEM)
     half_shape = jax.ShapeDtypeStruct((rows, 128), jnp.bfloat16)
 
-    def scalars(level):
+    def scalars(level, piece):
         bit = ap >> level & 1
-        return jnp.stack([first_row, jnp.int32(total_rows), bit]).astype(jnp.int32)
+        start = first_row + piece * (piece_bins // PH)
+        return jnp.stack([start, jnp.int32(total_rows), bit]).astype(jnp.int32)
 
     padded = with_halo(echoes, "range", 2, halo)
     padded = jnp.pad(padded, ((0, 0), (0, 0), (0, length - padded.shape[2])))
@@ -163,15 +164,21 @@
     toep = jnp.tile(ring, (1, BLOCK))[:, : BLOCK * window].reshape(2, BLOCK // PH, PH, window)
     toep = toep.transpose(0, 2, 1, 3).reshape(2, BLOCK, window)
 
-    kept, sent = pl.pallas_call(
-        functools.partial(compress_kernel, blocks, window),
-        out_shape=(half_shape, half_shape),
-        in_specs=[sm, vm, vm],
-        out_specs=(vm, vm),
-        scratch_shapes=[pltpu.VMEM((rows, 256), jnp.float32)],
-        compiler_params=PARAMS,
-        name="compress",
-    )(scalars(0), e_t, toep)
+    chains = []
+    for piece in range(PIECES):
+        kept, sent = pl.pallas_call(
+            functools.partial(compress_kernel, piece * (piece_bins // BLOCK), blocks, window),
+            out_shape=(half_shape, half_shape),
+            in_specs=[sm, vm, vm],
+            out_specs=(vm, vm),
+            scratch_shapes=[pltpu.VMEM((blocks * (BLOCK // PH), 256), jnp.float32)],
+            compiler_params=PARAMS,
+            cost_estimate=pl.CostEstimate(
+                flops=2 * blocks * BLOCK * window * 2 * 256, bytes_accessed=2**21, transcendentals=0
+            ),
+            name="compress",
+        )(scalars(0, piece), e_t, toep)
+        chains.append((kept, partner(sent, "aperture", 0)))
 
     side = jnp.stack([ap >> level & 1 for level in range(LEVELS)])
     live = jnp.arange(KERN, dtype=jnp.int32) < band_widths[..., None]
@@ -195,32 +202,41 @@
         + jnp.arange(PH, dtype=jnp.int32)[:, None, None]
     ).astype(jnp.bfloat16)
 
+    flops = 2 * rows * STEPS * 2 * 256 * 256
     for level in range(LEVELS):
-        received = partner(sent, "aperture", level)
         last = level == LEVELS - 1
-        operands = [scalars(level + 1), kept, received, wl[level], off[level], child[level]]
-        if last:
-            operands.append(perm)
-        result = pl.pallas_call(
-            functools.partial(merge_kernel, last, range_bins // PH),
-            out_shape=jax.ShapeDtypeStruct(echoes.shape, jnp.bfloat16)
-            if last
-            else (half_shape, half_shape),
-            in_specs=[sm] + [vm] * (len(operands) - 1),
-            out_specs=vm if last else (vm, vm),
-            scratch_shapes=[
-                pltpu.VMEM((rows + 16, 256), jnp.float32),
-                pltpu.VMEM((rows, 256), jnp.float32),
-                pltpu.VMEM((8, 56, 256), jnp.float32),
-                pltpu.VMEM((STEPS, 256, 256), jnp.bfloat16),
-                pltpu.VMEM((STEPS, 256, 256), jnp.bfloat16),
-            ],
-            compiler_params=PARAMS,
-            name="merge_last" if last else "merge",
-        )(*operands)
-        if last:
-            return result
-        kept, sent = result
+        for piece in range(PIECES):
+            kept, received = chains[piece]
+            operands = [scalars(level + 1, piece), kept, received]
+            operands += [wl[level], off[level], child[level]]
+            if last:
+                operands.append(perm)
+            result = pl.pallas_call(
+                functools.partial(merge_kernel, last, piece_bins // PH),
+                out_shape=jax.ShapeDtypeStruct(echoes.shape[:2] + (piece_bins,), jnp.bfloat16)
+                if last
+                else (half_shape, half_shape),
+                in_specs=[sm] + [vm] * (len(operands) - 1),
+                out_specs=vm if last else (vm, vm),
+                scratch_shapes=[
+                    pltpu.VMEM((rows + 16, 256), jnp.float32),
+                    pltpu.VMEM((rows, 256), jnp.float32),
+                    pltpu.VMEM((8, 56, 256), jnp.float32),
+                    pltpu.VMEM((STEPS, 256, 256), jnp.bfloat16),
+                    pltpu.VMEM((STEPS, 256, 256), jnp.bfloat16),
+                ],
+                compiler_params=PARAMS,
+                cost_estimate=pl.CostEstimate(
+                    flops=flops, bytes_accessed=2**21, transcendentals=0
+                ),
+                name="merge_last" if last else "merge",
+            )(*operands)
+            if last:
+                chains[piece] = result
+            else:
+                kept, sent = result
+                chains[piece] = (kept, partner(sent, "aperture", level + 1))
+    return jnp.concatenate(chains, axis=2)
 
 
 def solution(mesh):

time: 80 us -> 72.5 us (0.906)
  waiting for transfers between devices: 21.7 us -> 5.77 us
  Pallas kernels: 25.1 us -> 31.8 us
  starting transfers between devices: 12.7 us -> 16.2 us
  local copies, waits for them, and re-layouts: 16.1 us -> 13.7 us
  other arithmetic: 3.3 us -> 4.35 us
    ppermute x4 -> x8, waiting for transfers between devices: 21.6 us -> 5.77 us  [partner(): return lax.ppermute(block, axis, route)]
    pallas_call x5 -> x10, Pallas kernels: 25.1 us -> 31.8 us  [the longest x8 26.3 us: body(): pl.pallas_call(functools.partial(merge_kernel, last, piece_bins // PH), o...]
    ppermute x4 -> x8, starting transfers between devices: 5.95 us -> 10.1 us  [partner(): return lax.ppermute(block, axis, route)]
    concatenate x0 -> x1, other arithmetic: none -> 0.84 us  [body(): return jnp.concatenate(chains, axis=2)]
  transfers between devices with their start and end apart: 6 -> 10, of which waited for: 3 -> 2; matrix products, arithmetic and copies ran while one was open for 16% -> 17% of each run, Pallas kernels for 0% -> 34%
where the time goes in v2:
time: 72.5 us; the launch traced here: 72.2 us
  Pallas kernels  31.8 us (44%)
  starting transfers between devices  16.2 us (22%)
  local copies, waits for them, and re-layouts  13.7 us (19%)
  waiting for transfers between devices  5.77 us (8%)
  other arithmetic  4.35 us (6%)
    pallas_call x8, Pallas kernels, body(): pl.pallas_call(functools.partial(merge_kernel, last, piece_bins // PH), o...  26.3 us
    ppermute x8, starting transfers between devices, partner(): return lax.ppermute(block, axis, route)  10.1 us
    ppermute x8, waiting for transfers between devices, partner(): return lax.ppermute(block, axis, route)  5.77 us
    pallas_call x2, Pallas kernels, body(): pl.pallas_call(functools.partial(compress_kernel, piece * (piece_bins //...  5.52 us
    ppermute x1, starting transfers between devices, with_halo(): lax.ppermute(tail, axis, [(i, (i + 1) % count) for i in range(ends)])  4.84 us
    broadcast_in_dim x8, local copies, waits for them, and re-layouts, body(): jnp.broadcast_to(wl, (LEVELS, 2, 2, KERN, 2, PH, 2, HALF))  3.45 us
    another operation x2, local copies, waits for them, and re-layouts, body(): jnp.tile(ring, (1, BLOCK))[:, :BLOCK * window]  2.47 us
    reshape x1, local copies, waits for them, and re-layouts, body(): e_t = both.transpose(0, 2, 1, 3, 4).reshape(128, length).T  1.92 us
  transfers between devices with their start and end apart: 10, of which 2 were waited for; matrix products, arithmetic and copies ran while one was open for 17% of the time, Pallas kernels for 34%

profile of v2, /device:TPU:0, one launch (start us, length us, event | category | flops | bytes accessed | tf_op | source)
XLA Modules:
  0.0 72.2 jit_solution(15149733950514802345)
XLA Ops:
  0.0 0.9 %fusion.10 = (bf16[2,32,352]{2,1,0:T(8,128)(2,1)S(1)}, bf16[2,32,352]{2,1,0:T(8,128)(2,1)S(1)}) fusion(bf16[2,32,4096]{2,1,0:T(8,128)(2,1)} %param.6), kind=kLoop, calls=%fused_computation.55 | loop fusion | bytes 180224 | tf_op jit(solution)/shard_map/slice | solution.py:37
  0.9 4.8 %collective-permute-start = (bf16[2,32,352]{2,1,0:T(8,128)(2,1)S(1)}, bf16[2,32,352]{2,1,0:T(8,128)(2,1)S(1)}, u32[]{:S(2)}, u32[]{:S(2)}) collective-permute-start(bf16[2,32,352]{2,1,0:T(8,128)(2,1)S(1)} %get-tuple-element.48), channel_id=1, source_target_pairs={{0,1},{2,3},{4,5},{6,7},{8,9},{10,11},{12,13},{14,15},{16,17},{18,... | collective-permute-start | bytes 135176 | tf_op jit(solution)/shard_map/ppermute | solution.py:41
  5.8 1.3 %collective-permute-start.1 = (bf16[2,32,352]{2,1,0:T(8,128)(2,1)S(1)}, bf16[2,32,352]{2,1,0:T(8,128)(2,1)S(1)}, u32[]{:S(2)}, u32[]{:S(2)}) collective-permute-start(bf16[2,32,352]{2,1,0:T(8,128)(2,1)S(1)} %get-tuple-element.47), channel_id=1, source_target_pairs={{1,0},{3,2},{5,4},{7,6},{9,8},{11,10},{13,12},{15,14},{17,16},{19,... | collective-permute-start | bytes 135176 | tf_op jit(solution)/shard_map/ppermute | solution.py:43
  8.1 0.9 %broadcast_select_fusion = f32[4,2,2,32,16]{3,4,2,1,0:T(8,128)S(1)} fusion(f32[4,2,2,32,16]{3,4,2,1,0:T(8,128)} %param.8, pred[4,2,32,16]{2,3,1,0:T(8,128)(4,1)S(1)} %iota_compare_fusion.1), kind=kLoop, calls=%fused_computation.26 | loop fusion | flops 8192 | bytes 69632 | tf_op jit(solution)/shard_map/jit(_where)/select_n | solution.py:185
  10.9 2.4 %tile.10 = bf16[2,196864]{1,0:T(2,128)(2,1)S(1)} reshape(bf16[2,256,769]{2,1,0:T(8,128)(2,1)S(1)} %tile.4) | data formatting | bytes 1574912 | tf_op jit(solution)/shard_map/tile | solution.py:164
  20.6 1.1 %copy.21 = bf16[2,2,2,16,4864]{4,3,2,1,0:T(8,128)(2,1)} copy(bf16[2,2,2,16,4864]{4,3,1,2,0:T(8,128)(2,1)S(1)} %maximum_bitcast_fusion) | data formatting | bytes 2490368 | tf_op jit(solution)/shard_map/transpose | solution.py:161
  21.7 1.9 %copy.22 = bf16[128,4864]{0,1:T(8,128)(2,1)S(1)} copy(bf16[128,4864]{1,0:T(8,128)(2,1)} %bitcast.51) | data formatting | bytes 2490368 | tf_op jit(solution)/shard_map/reshape | solution.py:161
  23.7 2.8 %compress.3 = (bf16[560,128]{1,0:T(8,128)(2,1)S(1)}, bf16[560,128]{1,0:T(8,128)(2,1)S(1)}) custom-call(s32[3]{0:T(128)S(1)} %get-tuple-element.59.scal_ref, bf16[4864,128]{1,0:T(8,128)(2,1)S(1)} %bitcast.47, bf16[2,256,768]{2,1,0:T(8,128)(2,1)S(1)} %bitcast.49), custom_call_target="tpu_custom_call" | custom-call | flops 1811939328 | bytes 2097152 | tf_op jit(solution)/shard_map/compress/pallas_call | solution.py:169
  26.5 2.8 %compress.2 = (bf16[560,128]{1,0:T(8,128)(2,1)S(1)}, bf16[560,128]{1,0:T(8,128)(2,1)S(1)}) custom-call(s32[3]{0:T(128)S(1)} %get-tuple-element.60.scal_ref, bf16[4864,128]{1,0:T(8,128)(2,1)S(1)} %bitcast.48, bf16[2,256,768]{2,1,0:T(8,128)(2,1)S(1)} %bitcast.50), custom_call_target="tpu_custom_call" | custom-call | flops 1811939328 | bytes 2097152 | tf_op jit(solution)/shard_map/compress/pallas_call | solution.py:169
  29.8 2.8 %merge.9 = (bf16[560,128]{1,0:T(8,128)(2,1)S(1)}, bf16[560,128]{1,0:T(8,128)(2,1)S(1)}) custom-call(s32[3]{0:T(128)S(1)} %pad_add_fusion.8.refs_0_, bf16[560,128]{1,0:T(8,128)(2,1)S(1)} %get-tuple-element.29.refs_1_, bf16[560,128]{1,0:T(8,128)(2,1)S(1)} %collective-permute-done.6.refs_2_, f32[4,16,256]{2,1,0:T(8,128)S(1)} %broadcast_in_dim.97.refs_3_, ...), custom_call_target="tpu_custom_call" | custom-call | flops 1908408320 | bytes 2097152 | tf_op jit(solution)/shard_map/merge/pallas_call | solution.py:214
  32.7 1.6 %collective-permute-start.7 = (bf16[560,128]{1,0:T(8,128)(2,1)S(1)}, bf16[560,128]{1,0:T(8,128)(2,1)S(1)}, u32[]{:S(2)}, u32[]{:S(2)}) collective-permute-start(bf16[560,128]{1,0:T(8,128)(2,1)S(1)} %get-tuple-element.32), channel_id=1, source_target_pairs={{0,4},{4,0},{2,6},{6,2},{8,12},{12,8},{10,14},{14,10},{16,20},{20,... | collective-permute-start | bytes 430088 | tf_op jit(solution)/shard_map/ppermute | solution.py:31
  34.3 2.8 %merge.6 = (bf16[560,128]{1,0:T(8,128)(2,1)S(1)}, bf16[560,128]{1,0:T(8,128)(2,1)S(1)}) custom-call(s32[3]{0:T(128)S(1)} %pad_add_fusion.9.refs_0_, bf16[560,128]{1,0:T(8,128)(2,1)S(1)} %get-tuple-element.21.refs_1_, bf16[560,128]{1,0:T(8,128)(2,1)S(1)} %collective-permute-done.2.refs_2_, f32[4,16,256]{2,1,0:T(8,128)S(1)} %broadcast_in_dim.97.refs_3_, ...), custom_call_target="tpu_custom_call" | custom-call | flops 1908408320 | bytes 2097152 | tf_op jit(solution)/shard_map/merge/pallas_call | solution.py:214
  38.4 2.8 %merge.10 = (bf16[560,128]{1,0:T(8,128)(2,1)S(1)}, bf16[560,128]{1,0:T(8,128)(2,1)S(1)}) custom-call(s32[3]{0:T(128)S(1)} %pad_add_fusion.6.refs_0_, bf16[560,128]{1,0:T(8,128)(2,1)S(1)} %get-tuple-element.31.refs_1_, bf16[560,128]{1,0:T(8,128)(2,1)S(1)} %collective-permute-done.7.refs_2_, f32[4,16,256]{2,1,0:T(8,128)S(1)} %broadcast_in_dim.104.refs_3_, ...), custom_call_target="tpu_custom_call" | custom-call | flops 1908408320 | bytes 2097152 | tf_op jit(solution)/shard_map/merge/pallas_call | solution.py:214
  41.3 1.6 %collective-permute-start.8 = (bf16[560,128]{1,0:T(8,128)(2,1)S(1)}, bf16[560,128]{1,0:T(8,128)(2,1)S(1)}, u32[]{:S(2)}, u32[]{:S(2)}) collective-permute-start(bf16[560,128]{1,0:T(8,128)(2,1)S(1)} %get-tuple-element.34), channel_id=1, source_target_pairs={{0,8},{8,0},{2,10},{10,2},{4,12},{12,4},{6,14},{14,6},{16,24},{24,... | collective-permute-start | bytes 430088 | tf_op jit(solution)/shard_map/ppermute | solution.py:31
  42.9 3.1 %merge.7 = (bf16[560,128]{1,0:T(8,128)(2,1)S(1)}, bf16[560,128]{1,0:T(8,128)(2,1)S(1)}) custom-call(s32[3]{0:T(128)S(1)} %pad_add_fusion.7.refs_0_, bf16[560,128]{1,0:T(8,128)(2,1)S(1)} %get-tuple-element.23.refs_1_, bf16[560,128]{1,0:T(8,128)(2,1)S(1)} %collective-permute-done.3.refs_2_, f32[4,16,256]{2,1,0:T(8,128)S(1)} %broadcast_in_dim.104.refs_3_, ...), custom_call_target="tpu_custom_call" | custom-call | flops 1908408320 | bytes 2097152 | tf_op jit(solution)/shard_map/merge/pallas_call | solution.py:214
  46.0 1.3 %collective-permute-start.4 = (bf16[560,128]{1,0:T(8,128)(2,1)S(1)}, bf16[560,128]{1,0:T(8,128)(2,1)S(1)}, u32[]{:S(2)}, u32[]{:S(2)}) collective-permute-start(bf16[560,128]{1,0:T(8,128)(2,1)S(1)} %get-tuple-element.26), channel_id=1, source_target_pairs={{0,8},{8,0},{2,10},{10,2},{4,12},{12,4},{6,14},{14,6},{16,24},{24,... | collective-permute-start | bytes 430088 | tf_op jit(solution)/shard_map/ppermute | solution.py:31
  47.3 2.8 %merge.11 = (bf16[560,128]{1,0:T(8,128)(2,1)S(1)}, bf16[560,128]{1,0:T(8,128)(2,1)S(1)}) custom-call(s32[3]{0:T(128)S(1)} %pad_add_fusion.4.refs_0_, bf16[560,128]{1,0:T(8,128)(2,1)S(1)} %get-tuple-element.33.refs_1_, bf16[560,128]{1,0:T(8,128)(2,1)S(1)} %collective-permute-done.8.refs_2_, f32[4,16,256]{2,1,0:T(8,128)S(1)} %broadcast_in_dim.110.refs_3_, ...), custom_call_target="tpu_custom_call" | custom-call | flops 1908408320 | bytes 2097152 | tf_op jit(solution)/shard_map/merge/pallas_call | solution.py:214
  50.1 2.7 %collective-permute-start.9 = (bf16[560,128]{1,0:T(8,128)(2,1)S(1)}, bf16[560,128]{1,0:T(8,128)(2,1)S(1)}, u32[]{:S(2)}, u32[]{:S(2)}) collective-permute-start(bf16[560,128]{1,0:T(8,128)(2,1)S(1)} %get-tuple-element.36), channel_id=1, source_target_pairs={{0,16},{16,0},{2,18},{18,2},{4,20},{20,4},{6,22},{22,6},{8,24},{24... | collective-permute-start | bytes 430088 | tf_op jit(solution)/shard_map/ppermute | solution.py:31
  52.8 2.8 %merge.8 = (bf16[560,128]{1,0:T(8,128)(2,1)S(1)}, bf16[560,128]{1,0:T(8,128)(2,1)S(1)}) custom-call(s32[3]{0:T(128)S(1)} %pad_add_fusion.5.refs_0_, bf16[560,128]{1,0:T(8,128)(2,1)S(1)} %get-tuple-element.25.refs_1_, bf16[560,128]{1,0:T(8,128)(2,1)S(1)} %collective-permute-done.4.refs_2_, f32[4,16,256]{2,1,0:T(8,128)S(1)} %broadcast_in_dim.110.refs_3_, ...), custom_call_target="tpu_custom_call" | custom-call | flops 1908408320 | bytes 2097152 | tf_op jit(solution)/shard_map/merge/pallas_call | solution.py:214
  55.6 1.7 %collective-permute-start.5 = (bf16[560,128]{1,0:T(8,128)(2,1)S(1)}, bf16[560,128]{1,0:T(8,128)(2,1)S(1)}, u32[]{:S(2)}, u32[]{:S(2)}) collective-permute-start(bf16[560,128]{1,0:T(8,128)(2,1)S(1)} %get-tuple-element.28), channel_id=1, source_target_pairs={{0,16},{16,0},{2,18},{18,2},{4,20},{20,4},{6,22},{22,6},{8,24},{24... | collective-permute-start | bytes 430088 | tf_op jit(solution)/shard_map/ppermute | solution.py:31
  57.3 5.0 %collective-permute-done.9.refs_2_ = bf16[560,128]{1,0:T(8,128)(2,1)S(1)} collective-permute-done((bf16[560,128]{1,0:T(8,128)(2,1)S(1)}, bf16[560,128]{1,0:T(8,128)(2,1)S(1)}, u32[]{:S(2)}, u32[]{:S(2)}) %collective-permute-start.9) | collective-permute-done | bytes 143392 | tf_op jit(solution)/shard_map/ppermute | solution.py:31
  62.3 4.5 %merge_last.3 = bf16[2,32,2048]{2,1,0:T(8,128)(2,1)S(1)} custom-call(s32[3]{0:T(128)S(1)} %get-tuple-element.57.refs_0_, bf16[560,128]{1,0:T(8,128)(2,1)S(1)} %get-tuple-element.35.refs_1_, bf16[560,128]{1,0:T(8,128)(2,1)S(1)} %collective-permute-done.9.refs_2_, f32[4,16,256]{2,1,0:T(8,128)S(1)} %broadcast_in_dim.116.refs_3_, ...), custom_call_target="tpu_custom_call" | custom-call | flops 1908408320 | bytes 2097152 | tf_op jit(solution)/shard_map/merge_last/pallas_call | solution.py:214
  66.9 4.5 %merge_last.2 = bf16[2,32,2048]{2,1,0:T(8,128)(2,1)S(1)} custom-call(s32[3]{0:T(128)S(1)} %get-tuple-element.58.refs_0_, bf16[560,128]{1,0:T(8,128)(2,1)S(1)} %get-tuple-element.27.refs_1_, bf16[560,128]{1,0:T(8,128)(2,1)S(1)} %collective-permute-done.5.refs_2_, f32[4,16,256]{2,1,0:T(8,128)S(1)} %broadcast_in_dim.116.refs_3_, ...), custom_call_target="tpu_custom_call" | custom-call | flops 1908408320 | bytes 2097152 | tf_op jit(solution)/shard_map/merge_last/pallas_call | solution.py:214
  71.4 0.8 %pad_maximum_fusion.1 = bf16[2,32,4096]{2,1,0:T(8,128)(2,1)} fusion(bf16[2,32,2048]{2,1,0:T(8,128)(2,1)S(1)} %merge_last.3, bf16[2,32,2048]{2,1,0:T(8,128)(2,1)S(1)} %merge_last.2), kind=kLoop, calls=%fused_computation.10 | loop fusion | flops 1048576 | bytes 1048576 | tf_op jit(solution)/shard_map/concatenate | solution.py:239
  (87 shorter events, 11.8 us)
Async XLA Ops:
  0.0 9.8 %copy-start.1 = (s32[4,2,32]{2,1,0:T(2,128)S(1)}, s32[4,2,32]{2,1,0:T(2,128)}, u32[]{:S(2)}) copy-start(s32[4,2,32]{2,1,0:T(2,128)} %param.9) | copy-start | bytes 3076
  0.0 10.0 %copy-start.3 = (s32[4,32]{1,0:T(4,128)S(1)}, s32[4,32]{1,0:T(4,128)}, u32[]{:S(2)}) copy-start(s32[4,32]{1,0:T(4,128)} %param.11) | copy-start | bytes 1540
  0.9 18.7 %collective-permute-start = (bf16[2,32,352]{2,1,0:T(8,128)(2,1)S(1)}, bf16[2,32,352]{2,1,0:T(8,128)(2,1)S(1)}, u32[]{:S(2)}, u32[]{:S(2)}) collective-permute-start(bf16[2,32,352]{2,1,0:T(8,128)(2,1)S(1)} %get-tuple-element.48), channel_id=1, source_target_pairs={{0,1},{2,3},{4,5},{6,7},{8,9},{10,11},{12,13},{14,15},{16,17},{18,... | collective-permute-start | bytes 135176 | tf_op jit(solution)/shard_map/ppermute | solution.py:41
  5.8 13.8 %collective-permute-start.1 = (bf16[2,32,352]{2,1,0:T(8,128)(2,1)S(1)}, bf16[2,32,352]{2,1,0:T(8,128)(2,1)S(1)}, u32[]{:S(2)}, u32[]{:S(2)}) collective-permute-start(bf16[2,32,352]{2,1,0:T(8,128)(2,1)S(1)} %get-tuple-element.47), channel_id=1, source_target_pairs={{1,0},{3,2},{5,4},{7,6},{9,8},{11,10},{13,12},{15,14},{17,16},{19,... | collective-permute-start | bytes 135176 | tf_op jit(solution)/shard_map/ppermute | solution.py:43
  10.0 0.8 %copy-start.2 = (bf16[2,512]{1,0:T(2,128)(2,1)S(1)}, bf16[2,512]{1,0:T(2,128)(2,1)}, u32[]{:S(2)}) copy-start(bf16[2,512]{1,0:T(2,128)(2,1)} %param.7) | copy-start | bytes 6148
  17.3 2.3 %copy-start = (bf16[2,32,4096]{2,1,0:T(8,128)(2,1)S(1)}, bf16[2,32,4096]{2,1,0:T(8,128)(2,1)}, u32[]{:S(2)}) copy-start(bf16[2,32,4096]{2,1,0:T(8,128)(2,1)} %param.6) | copy-start | bytes 1572868
  26.4 3.4 %collective-permute-start.6 = (bf16[560,128]{1,0:T(8,128)(2,1)S(1)}, bf16[560,128]{1,0:T(8,128)(2,1)S(1)}, u32[]{:S(2)}, u32[]{:S(2)}) collective-permute-start(bf16[560,128]{1,0:T(8,128)(2,1)S(1)} %get-tuple-element.30), channel_id=1, source_target_pairs={{0,2},{2,0},{4,6},{6,4},{8,10},{10,8},{12,14},{14,12},{16,18},{18,... | collective-permute-start | bytes 430088 | tf_op jit(solution)/shard_map/ppermute | solution.py:31
  29.3 5.0 %collective-permute-start.2 = (bf16[560,128]{1,0:T(8,128)(2,1)S(1)}, bf16[560,128]{1,0:T(8,128)(2,1)S(1)}, u32[]{:S(2)}, u32[]{:S(2)}) collective-permute-start(bf16[560,128]{1,0:T(8,128)(2,1)S(1)} %get-tuple-element.22), channel_id=1, source_target_pairs={{0,2},{2,0},{4,6},{6,4},{8,10},{10,8},{12,14},{14,12},{16,18},{18,... | collective-permute-start | bytes 430088 | tf_op jit(solution)/shard_map/ppermute | solution.py:31
  32.7 5.7 %collective-permute-start.7 = (bf16[560,128]{1,0:T(8,128)(2,1)S(1)}, bf16[560,128]{1,0:T(8,128)(2,1)S(1)}, u32[]{:S(2)}, u32[]{:S(2)}) collective-permute-start(bf16[560,128]{1,0:T(8,128)(2,1)S(1)} %get-tuple-element.32), channel_id=1, source_target_pairs={{0,4},{4,0},{2,6},{6,2},{8,12},{12,8},{10,14},{14,10},{16,20},{20,... | collective-permute-start | bytes 430088 | tf_op jit(solution)/shard_map/ppermute | solution.py:31
  37.1 5.8 %collective-permute-start.3 = (bf16[560,128]{1,0:T(8,128)(2,1)S(1)}, bf16[560,128]{1,0:T(8,128)(2,1)S(1)}, u32[]{:S(2)}, u32[]{:S(2)}) collective-permute-start(bf16[560,128]{1,0:T(8,128)(2,1)S(1)} %get-tuple-element.24), channel_id=1, source_target_pairs={{0,4},{4,0},{2,6},{6,2},{8,12},{12,8},{10,14},{14,10},{16,20},{20,... | collective-permute-start | bytes 430088 | tf_op jit(solution)/shard_map/ppermute | solution.py:31
  41.3 6.0 %collective-permute-start.8 = (bf16[560,128]{1,0:T(8,128)(2,1)S(1)}, bf16[560,128]{1,0:T(8,128)(2,1)S(1)}, u32[]{:S(2)}, u32[]{:S(2)}) collective-permute-start(bf16[560,128]{1,0:T(8,128)(2,1)S(1)} %get-tuple-element.34), channel_id=1, source_target_pairs={{0,8},{8,0},{2,10},{10,2},{4,12},{12,4},{6,14},{14,6},{16,24},{24,... | collective-permute-start | bytes 430088 | tf_op jit(solution)/shard_map/ppermute | solution.py:31
  46.0 6.8 %collective-permute-start.4 = (bf16[560,128]{1,0:T(8,128)(2,1)S(1)}, bf16[560,128]{1,0:T(8,128)(2,1)S(1)}, u32[]{:S(2)}, u32[]{:S(2)}) collective-permute-start(bf16[560,128]{1,0:T(8,128)(2,1)S(1)} %get-tuple-element.26), channel_id=1, source_target_pairs={{0,8},{8,0},{2,10},{10,2},{4,12},{12,4},{6,14},{14,6},{16,24},{24,... | collective-permute-start | bytes 430088 | tf_op jit(solution)/shard_map/ppermute | solution.py:31
  50.1 12.2 %collective-permute-start.9 = (bf16[560,128]{1,0:T(8,128)(2,1)S(1)}, bf16[560,128]{1,0:T(8,128)(2,1)S(1)}, u32[]{:S(2)}, u32[]{:S(2)}) collective-permute-start(bf16[560,128]{1,0:T(8,128)(2,1)S(1)} %get-tuple-element.36), channel_id=1, source_target_pairs={{0,16},{16,0},{2,18},{18,2},{4,20},{20,4},{6,22},{22,6},{8,24},{24... | collective-permute-start | bytes 430088 | tf_op jit(solution)/shard_map/ppermute | solution.py:31
  55.6 11.2 %collective-permute-start.5 = (bf16[560,128]{1,0:T(8,128)(2,1)S(1)}, bf16[560,128]{1,0:T(8,128)(2,1)S(1)}, u32[]{:S(2)}, u32[]{:S(2)}) collective-permute-start(bf16[560,128]{1,0:T(8,128)(2,1)S(1)} %get-tuple-element.28), channel_id=1, source_target_pairs={{0,16},{16,0},{2,18},{18,2},{4,20},{20,4},{6,22},{22,6},{8,24},{24... | collective-permute-start | bytes 430088 | tf_op jit(solution)/shard_map/ppermute | solution.py:31

commit v3 on v2

--- a/solution.py
+++ b/solution.py
@@ -56,8 +56,13 @@
     sent_ref[...] = jnp.where(upper, first, second).astype(jnp.bfloat16)
 
 
-def compress_kernel(start, blocks, window, scal_ref, e_ref, t_ref, kept_ref, sent_ref, y_ref):
+def compress_kernel(start, blocks, window, scal_ref, e_ref, c_ref, kept_ref, sent_ref, y_ref, t_ref):
     rows = BLOCK // PH
+    for ri in range(2):
+        ring = jnp.broadcast_to(c_ref[ri : ri + 1, :], (rows, window))
+        for po in range(PH):
+            turned = pltpu.roll(ring, po, 1, stride=PH, stride_axis=0)
+            t_ref[ri, po * rows : (po + 1) * rows, :] = turned.astype(jnp.bfloat16)
     for b in range(blocks):
         w = e_ref[(start + b) * BLOCK : (start + b) * BLOCK + window, :]
         acc = jnp.dot(t_ref[0], w[:, :64], preferred_element_type=jnp.float32)
@@ -160,9 +165,7 @@
     both = jnp.stack([padded, turned]).reshape(2, 2, 2, HALF, length)
     e_t = both.transpose(0, 2, 1, 3, 4).reshape(128, length).T
 
-    ring = jnp.pad(transmit_chirp, ((0, 0), (0, window + 1 - taps)))
-    toep = jnp.tile(ring, (1, BLOCK))[:, : BLOCK * window].reshape(2, BLOCK // PH, PH, window)
-    toep = toep.transpose(0, 2, 1, 3).reshape(2, BLOCK, window)
+    ring = jnp.pad(transmit_chirp.astype(jnp.float32), ((0, 0), (0, window - taps)))
 
     chains = []
     for piece in range(PIECES):
@@ -171,13 +174,16 @@
             out_shape=(half_shape, half_shape),
             in_specs=[sm, vm, vm],
             out_specs=(vm, vm),
-            scratch_shapes=[pltpu.VMEM((blocks * (BLOCK // PH), 256), jnp.float32)],
+            scratch_shapes=[
+                pltpu.VMEM((blocks * (BLOCK // PH), 256), jnp.float32),
+                pltpu.VMEM((2, BLOCK, window), jnp.bfloat16),
+            ],
             compiler_params=PARAMS,
             cost_estimate=pl.CostEstimate(
                 flops=2 * blocks * BLOCK * window * 2 * 256, bytes_accessed=2**21, transcendentals=0
             ),
             name="compress",
-        )(scalars(0, piece), e_t, toep)
+        )(scalars(0, piece), e_t, ring)
         chains.append((kept, partner(sent, "aperture", 0)))
 
     side = jnp.stack([ap >> level & 1 for level in range(LEVELS)])

time: 72.5 us -> 66.6 us (0.919)
  local copies, waits for them, and re-layouts: 13.7 us -> 7.99 us
    another operation x2 -> x0, local copies, waits for them, and re-layouts: 2.47 us -> none  [body(): jnp.tile(ring, (1, BLOCK))[:, :BLOCK * window]]
    transpose x1, local copies, waits for them, and re-layouts: 1.13 us -> 0.08 us  [body(): e_t = both.transpose(0, 2, 1, 3, 4).reshape(128, length).T]
    reshape x1, local copies, waits for them, and re-layouts: 1.92 us -> 0.96 us  [body(): e_t = both.transpose(0, 2, 1, 3, 4).reshape(128, length).T]
  transfers between devices with their start and end apart: 10 -> 10, of which waited for: 2 -> 2; matrix products, arithmetic and copies ran while one was open for 17% -> 13% of each run, Pallas kernels for 34% -> 37%
where the time goes in v3:
time: 66.6 us; the launch traced here: 66.3 us
  Pallas kernels  31.6 us (47%)
  starting transfers between devices  16.2 us (24%)
  local copies, waits for them, and re-layouts  7.99 us (12%)
  waiting for transfers between devices  5.77 us (9%)
  other arithmetic  4.32 us (6%)
    pallas_call x8, Pallas kernels, body(): pl.pallas_call(functools.partial(merge_kernel, last, piece_bins // PH), o...  26.2 us
    ppermute x8, starting transfers between devices, partner(): return lax.ppermute(block, axis, route)  10.1 us
    ppermute x8, waiting for transfers between devices, partner(): return lax.ppermute(block, axis, route)  5.76 us
    pallas_call x2, Pallas kernels, body(): pl.pallas_call(functools.partial(compress_kernel, piece * (piece_bins //...  5.4 us
    ppermute x1, starting transfers between devices, with_halo(): lax.ppermute(tail, axis, [(i, (i + 1) % count) for i in range(ends)])  4.84 us
    broadcast_in_dim x8, local copies, waits for them, and re-layouts, body(): jnp.broadcast_to(wl, (LEVELS, 2, 2, KERN, 2, PH, 2, HALF))  3.41 us
  transfers between devices with their start and end apart: 10, of which 2 were waited for; matrix products, arithmetic and copies ran while one was open for 13% of the time, Pallas kernels for 37%

profile of v3, /device:TPU:0, one launch (start us, length us, event | category | flops | bytes accessed | tf_op | source)
XLA Modules:
  0.0 66.3 jit_solution(3702788780683502001)
XLA Ops:
  0.0 0.9 %fusion.10 = (bf16[2,32,352]{2,1,0:T(8,128)(2,1)S(1)}, bf16[2,32,352]{2,1,0:T(8,128)(2,1)S(1)}) fusion(bf16[2,32,4096]{2,1,0:T(8,128)(2,1)} %param.6), kind=kLoop, calls=%fused_computation.56 | loop fusion | bytes 180224 | tf_op jit(solution)/shard_map/slice | solution.py:37
  1.0 4.8 %collective-permute-start = (bf16[2,32,352]{2,1,0:T(8,128)(2,1)S(1)}, bf16[2,32,352]{2,1,0:T(8,128)(2,1)S(1)}, u32[]{:S(2)}, u32[]{:S(2)}) collective-permute-start(bf16[2,32,352]{2,1,0:T(8,128)(2,1)S(1)} %get-tuple-element.48), channel_id=1, source_target_pairs={{0,1},{2,3},{4,5},{6,7},{8,9},{10,11},{12,13},{14,15},{16,17},{18,... | collective-permute-start | bytes 135176 | tf_op jit(solution)/shard_map/ppermute | solution.py:41
  5.8 1.3 %collective-permute-start.1 = (bf16[2,32,352]{2,1,0:T(8,128)(2,1)S(1)}, bf16[2,32,352]{2,1,0:T(8,128)(2,1)S(1)}, u32[]{:S(2)}, u32[]{:S(2)}) collective-permute-start(bf16[2,32,352]{2,1,0:T(8,128)(2,1)S(1)} %get-tuple-element.47), channel_id=1, source_target_pairs={{1,0},{3,2},{5,4},{7,6},{9,8},{11,10},{13,12},{15,14},{17,16},{19,... | collective-permute-start | bytes 135176 | tf_op jit(solution)/shard_map/ppermute | solution.py:43
  8.1 0.9 %broadcast_select_fusion = f32[4,2,2,32,16]{3,4,2,1,0:T(8,128)S(1)} fusion(f32[4,2,2,32,16]{3,4,2,1,0:T(8,128)} %param.8, pred[4,2,32,16]{2,3,1,0:T(8,128)(4,1)S(1)} %iota_compare_fusion.1), kind=kLoop, calls=%fused_computation.26 | loop fusion | flops 8192 | bytes 69632 | tf_op jit(solution)/shard_map/jit(_where)/select_n | solution.py:191
  11.1 0.7 %broadcast_in_dim.97.refs_3_ = f32[4,16,256]{2,1,0:T(8,128)S(1)} reshape(f32[2,2,16,2,4,2,16]{6,5,4,3,2,1,0:T(2,128)S(1)} %broadcast_in_dim.96) | data formatting | bytes 131072 | tf_op jit(solution)/shard_map/broadcast_in_dim | solution.py:198
  17.0 1.0 %copy.21 = bf16[128,4864]{0,1:T(8,128)(2,1)S(1)} copy(bf16[128,4864]{1,0:T(8,128)(2,1)S(1)} %bitcast.47) | data formatting | bytes 2490368 | tf_op jit(solution)/shard_map/reshape | solution.py:166
  17.9 2.7 %compress.3 = (bf16[560,128]{1,0:T(8,128)(2,1)S(1)}, bf16[560,128]{1,0:T(8,128)(2,1)S(1)}) custom-call(s32[3]{0:T(128)S(1)} %get-tuple-element.59.scal_ref, bf16[4864,128]{1,0:T(8,128)(2,1)S(1)} %bitcast.45, f32[2,768]{1,0:T(2,128)S(1)} %pad_convert_fusion.c_ref), custom_call_target="tpu_custom_call" | custom-call | flops 1811939328 | bytes 2097152 | tf_op jit(solution)/shard_map/compress/pallas_call | solution.py:172
  20.7 2.7 %compress.2 = (bf16[560,128]{1,0:T(8,128)(2,1)S(1)}, bf16[560,128]{1,0:T(8,128)(2,1)S(1)}) custom-call(s32[3]{0:T(128)S(1)} %get-tuple-element.60.scal_ref, bf16[4864,128]{1,0:T(8,128)(2,1)S(1)} %bitcast.46, f32[2,768]{1,0:T(2,128)S(1)} %pad_convert_fusion.c_ref), custom_call_target="tpu_custom_call" | custom-call | flops 1811939328 | bytes 2097152 | tf_op jit(solution)/shard_map/compress/pallas_call | solution.py:172
  24.0 2.8 %merge.9 = (bf16[560,128]{1,0:T(8,128)(2,1)S(1)}, bf16[560,128]{1,0:T(8,128)(2,1)S(1)}) custom-call(s32[3]{0:T(128)S(1)} %pad_add_fusion.8.refs_0_, bf16[560,128]{1,0:T(8,128)(2,1)S(1)} %get-tuple-element.29.refs_1_, bf16[560,128]{1,0:T(8,128)(2,1)S(1)} %collective-permute-done.6.refs_2_, f32[4,16,256]{2,1,0:T(8,128)S(1)} %broadcast_in_dim.97.refs_3_, ...), custom_call_target="tpu_custom_call" | custom-call | flops 1908408320 | bytes 2097152 | tf_op jit(solution)/shard_map/merge/pallas_call | solution.py:220
  26.8 1.6 %collective-permute-start.7 = (bf16[560,128]{1,0:T(8,128)(2,1)S(1)}, bf16[560,128]{1,0:T(8,128)(2,1)S(1)}, u32[]{:S(2)}, u32[]{:S(2)}) collective-permute-start(bf16[560,128]{1,0:T(8,128)(2,1)S(1)} %get-tuple-element.32), channel_id=1, source_target_pairs={{0,4},{4,0},{2,6},{6,2},{8,12},{12,8},{10,14},{14,10},{16,20},{20,... | collective-permute-start | bytes 430088 | tf_op jit(solution)/shard_map/ppermute | solution.py:31
  28.4 2.8 %merge.6 = (bf16[560,128]{1,0:T(8,128)(2,1)S(1)}, bf16[560,128]{1,0:T(8,128)(2,1)S(1)}) custom-call(s32[3]{0:T(128)S(1)} %pad_add_fusion.9.refs_0_, bf16[560,128]{1,0:T(8,128)(2,1)S(1)} %get-tuple-element.21.refs_1_, bf16[560,128]{1,0:T(8,128)(2,1)S(1)} %collective-permute-done.2.refs_2_, f32[4,16,256]{2,1,0:T(8,128)S(1)} %broadcast_in_dim.97.refs_3_, ...), custom_call_target="tpu_custom_call" | custom-call | flops 1908408320 | bytes 2097152 | tf_op jit(solution)/shard_map/merge/pallas_call | solution.py:220
  31.8 0.8 %collective-permute-done.7.refs_2_ = bf16[560,128]{1,0:T(8,128)(2,1)S(1)} collective-permute-done((bf16[560,128]{1,0:T(8,128)(2,1)S(1)}, bf16[560,128]{1,0:T(8,128)(2,1)S(1)}, u32[]{:S(2)}, u32[]{:S(2)}) %collective-permute-start.7) | collective-permute-done | bytes 143392 | tf_op jit(solution)/shard_map/ppermute | solution.py:31
  32.6 2.8 %merge.10 = (bf16[560,128]{1,0:T(8,128)(2,1)S(1)}, bf16[560,128]{1,0:T(8,128)(2,1)S(1)}) custom-call(s32[3]{0:T(128)S(1)} %pad_add_fusion.6.refs_0_, bf16[560,128]{1,0:T(8,128)(2,1)S(1)} %get-tuple-element.31.refs_1_, bf16[560,128]{1,0:T(8,128)(2,1)S(1)} %collective-permute-done.7.refs_2_, f32[4,16,256]{2,1,0:T(8,128)S(1)} %broadcast_in_dim.104.refs_3_, ...), custom_call_target="tpu_custom_call" | custom-call | flops 1908408320 | bytes 2097152 | tf_op jit(solution)/shard_map/merge/pallas_call | solution.py:220
  35.4 1.6 %collective-permute-start.8 = (bf16[560,128]{1,0:T(8,128)(2,1)S(1)}, bf16[560,128]{1,0:T(8,128)(2,1)S(1)}, u32[]{:S(2)}, u32[]{:S(2)}) collective-permute-start(bf16[560,128]{1,0:T(8,128)(2,1)S(1)} %get-tuple-element.34), channel_id=1, source_target_pairs={{0,8},{8,0},{2,10},{10,2},{4,12},{12,4},{6,14},{14,6},{16,24},{24,... | collective-permute-start | bytes 430088 | tf_op jit(solution)/shard_map/ppermute | solution.py:31
  37.0 3.1 %merge.7 = (bf16[560,128]{1,0:T(8,128)(2,1)S(1)}, bf16[560,128]{1,0:T(8,128)(2,1)S(1)}) custom-call(s32[3]{0:T(128)S(1)} %pad_add_fusion.7.refs_0_, bf16[560,128]{1,0:T(8,128)(2,1)S(1)} %get-tuple-element.23.refs_1_, bf16[560,128]{1,0:T(8,128)(2,1)S(1)} %collective-permute-done.3.refs_2_, f32[4,16,256]{2,1,0:T(8,128)S(1)} %broadcast_in_dim.104.refs_3_, ...), custom_call_target="tpu_custom_call" | custom-call | flops 1908408320 | bytes 2097152 | tf_op jit(solution)/shard_map/merge/pallas_call | solution.py:220
  40.1 1.3 %collective-permute-start.4 = (bf16[560,128]{1,0:T(8,128)(2,1)S(1)}, bf16[560,128]{1,0:T(8,128)(2,1)S(1)}, u32[]{:S(2)}, u32[]{:S(2)}) collective-permute-start(bf16[560,128]{1,0:T(8,128)(2,1)S(1)} %get-tuple-element.26), channel_id=1, source_target_pairs={{0,8},{8,0},{2,10},{10,2},{4,12},{12,4},{6,14},{14,6},{16,24},{24,... | collective-permute-start | bytes 430088 | tf_op jit(solution)/shard_map/ppermute | solution.py:31
  41.4 2.8 %merge.11 = (bf16[560,128]{1,0:T(8,128)(2,1)S(1)}, bf16[560,128]{1,0:T(8,128)(2,1)S(1)}) custom-call(s32[3]{0:T(128)S(1)} %pad_add_fusion.4.refs_0_, bf16[560,128]{1,0:T(8,128)(2,1)S(1)} %get-tuple-element.33.refs_1_, bf16[560,128]{1,0:T(8,128)(2,1)S(1)} %collective-permute-done.8.refs_2_, f32[4,16,256]{2,1,0:T(8,128)S(1)} %broadcast_in_dim.110.refs_3_, ...), custom_call_target="tpu_custom_call" | custom-call | flops 1908408320 | bytes 2097152 | tf_op jit(solution)/shard_map/merge/pallas_call | solution.py:220
  44.2 2.6 %collective-permute-start.9 = (bf16[560,128]{1,0:T(8,128)(2,1)S(1)}, bf16[560,128]{1,0:T(8,128)(2,1)S(1)}, u32[]{:S(2)}, u32[]{:S(2)}) collective-permute-start(bf16[560,128]{1,0:T(8,128)(2,1)S(1)} %get-tuple-element.36), channel_id=1, source_target_pairs={{0,16},{16,0},{2,18},{18,2},{4,20},{20,4},{6,22},{22,6},{8,24},{24... | collective-permute-start | bytes 430088 | tf_op jit(solution)/shard_map/ppermute | solution.py:31
  46.9 2.8 %merge.8 = (bf16[560,128]{1,0:T(8,128)(2,1)S(1)}, bf16[560,128]{1,0:T(8,128)(2,1)S(1)}) custom-call(s32[3]{0:T(128)S(1)} %pad_add_fusion.5.refs_0_, bf16[560,128]{1,0:T(8,128)(2,1)S(1)} %get-tuple-element.25.refs_1_, bf16[560,128]{1,0:T(8,128)(2,1)S(1)} %collective-permute-done.4.refs_2_, f32[4,16,256]{2,1,0:T(8,128)S(1)} %broadcast_in_dim.110.refs_3_, ...), custom_call_target="tpu_custom_call" | custom-call | flops 1908408320 | bytes 2097152 | tf_op jit(solution)/shard_map/merge/pallas_call | solution.py:220
  49.7 1.7 %collective-permute-start.5 = (bf16[560,128]{1,0:T(8,128)(2,1)S(1)}, bf16[560,128]{1,0:T(8,128)(2,1)S(1)}, u32[]{:S(2)}, u32[]{:S(2)}) collective-permute-start(bf16[560,128]{1,0:T(8,128)(2,1)S(1)} %get-tuple-element.28), channel_id=1, source_target_pairs={{0,16},{16,0},{2,18},{18,2},{4,20},{20,4},{6,22},{22,6},{8,24},{24... | collective-permute-start | bytes 430088 | tf_op jit(solution)/shard_map/ppermute | solution.py:31
  51.4 5.0 %collective-permute-done.9.refs_2_ = bf16[560,128]{1,0:T(8,128)(2,1)S(1)} collective-permute-done((bf16[560,128]{1,0:T(8,128)(2,1)S(1)}, bf16[560,128]{1,0:T(8,128)(2,1)S(1)}, u32[]{:S(2)}, u32[]{:S(2)}) %collective-permute-start.9) | collective-permute-done | bytes 143392 | tf_op jit(solution)/shard_map/ppermute | solution.py:31
  56.4 4.5 %merge_last.3 = bf16[2,32,2048]{2,1,0:T(8,128)(2,1)S(1)} custom-call(s32[3]{0:T(128)S(1)} %get-tuple-element.57.refs_0_, bf16[560,128]{1,0:T(8,128)(2,1)S(1)} %get-tuple-element.35.refs_1_, bf16[560,128]{1,0:T(8,128)(2,1)S(1)} %collective-permute-done.9.refs_2_, f32[4,16,256]{2,1,0:T(8,128)S(1)} %broadcast_in_dim.116.refs_3_, ...), custom_call_target="tpu_custom_call" | custom-call | flops 1908408320 | bytes 2097152 | tf_op jit(solution)/shard_map/merge_last/pallas_call | solution.py:220
  61.0 4.5 %merge_last.2 = bf16[2,32,2048]{2,1,0:T(8,128)(2,1)S(1)} custom-call(s32[3]{0:T(128)S(1)} %get-tuple-element.58.refs_0_, bf16[560,128]{1,0:T(8,128)(2,1)S(1)} %get-tuple-element.27.refs_1_, bf16[560,128]{1,0:T(8,128)(2,1)S(1)} %collective-permute-done.5.refs_2_, f32[4,16,256]{2,1,0:T(8,128)S(1)} %broadcast_in_dim.116.refs_3_, ...), custom_call_target="tpu_custom_call" | custom-call | flops 1908408320 | bytes 2097152 | tf_op jit(solution)/shard_map/merge_last/pallas_call | solution.py:220
  65.5 0.8 %pad_maximum_fusion.1 = bf16[2,32,4096]{2,1,0:T(8,128)(2,1)} fusion(bf16[2,32,2048]{2,1,0:T(8,128)(2,1)S(1)} %merge_last.3, bf16[2,32,2048]{2,1,0:T(8,128)(2,1)S(1)} %merge_last.2), kind=kLoop, calls=%fused_computation.10 | loop fusion | flops 1048576 | bytes 1048576 | tf_op jit(solution)/shard_map/concatenate | solution.py:245
  (82 shorter events, 9.2 us)
Async XLA Ops:
  0.0 9.8 %copy-start.3 = (bf16[2,512]{1,0:T(2,128)(2,1)S(1)}, bf16[2,512]{1,0:T(2,128)(2,1)}, u32[]{:S(2)}) copy-start(bf16[2,512]{1,0:T(2,128)(2,1)} %param.7) | copy-start | bytes 6148
  0.0 9.8 %copy-start.1 = (s32[4,2,32]{2,1,0:T(2,128)S(1)}, s32[4,2,32]{2,1,0:T(2,128)}, u32[]{:S(2)}) copy-start(s32[4,2,32]{2,1,0:T(2,128)} %param.9) | copy-start | bytes 3076
  0.0 10.0 %copy-start.2 = (s32[4,32]{1,0:T(4,128)S(1)}, s32[4,32]{1,0:T(4,128)}, u32[]{:S(2)}) copy-start(s32[4,32]{1,0:T(4,128)} %param.11) | copy-start | bytes 1540
  1.0 14.9 %collective-permute-start = (bf16[2,32,352]{2,1,0:T(8,128)(2,1)S(1)}, bf16[2,32,352]{2,1,0:T(8,128)(2,1)S(1)}, u32[]{:S(2)}, u32[]{:S(2)}) collective-permute-start(bf16[2,32,352]{2,1,0:T(8,128)(2,1)S(1)} %get-tuple-element.48), channel_id=1, source_target_pairs={{0,1},{2,3},{4,5},{6,7},{8,9},{10,11},{12,13},{14,15},{16,17},{18,... | collective-permute-start | bytes 135176 | tf_op jit(solution)/shard_map/ppermute | solution.py:41
  5.8 10.1 %collective-permute-start.1 = (bf16[2,32,352]{2,1,0:T(8,128)(2,1)S(1)}, bf16[2,32,352]{2,1,0:T(8,128)(2,1)S(1)}, u32[]{:S(2)}, u32[]{:S(2)}) collective-permute-start(bf16[2,32,352]{2,1,0:T(8,128)(2,1)S(1)} %get-tuple-element.47), channel_id=1, source_target_pairs={{1,0},{3,2},{5,4},{7,6},{9,8},{11,10},{13,12},{15,14},{17,16},{19,... | collective-permute-start | bytes 135176 | tf_op jit(solution)/shard_map/ppermute | solution.py:43
  13.6 2.3 %copy-start = (bf16[2,32,4096]{2,1,0:T(8,128)(2,1)S(1)}, bf16[2,32,4096]{2,1,0:T(8,128)(2,1)}, u32[]{:S(2)}) copy-start(bf16[2,32,4096]{2,1,0:T(8,128)(2,1)} %param.6) | copy-start | bytes 1572868
  20.6 3.3 %collective-permute-start.6 = (bf16[560,128]{1,0:T(8,128)(2,1)S(1)}, bf16[560,128]{1,0:T(8,128)(2,1)S(1)}, u32[]{:S(2)}, u32[]{:S(2)}) collective-permute-start(bf16[560,128]{1,0:T(8,128)(2,1)S(1)} %get-tuple-element.30), channel_id=1, source_target_pairs={{0,2},{2,0},{4,6},{6,4},{8,10},{10,8},{12,14},{14,12},{16,18},{18,... | collective-permute-start | bytes 430088 | tf_op jit(solution)/shard_map/ppermute | solution.py:31
  23.4 5.0 %collective-permute-start.2 = (bf16[560,128]{1,0:T(8,128)(2,1)S(1)}, bf16[560,128]{1,0:T(8,128)(2,1)S(1)}, u32[]{:S(2)}, u32[]{:S(2)}) collective-permute-start(bf16[560,128]{1,0:T(8,128)(2,1)S(1)} %get-tuple-element.22), channel_id=1, source_target_pairs={{0,2},{2,0},{4,6},{6,4},{8,10},{10,8},{12,14},{14,12},{16,18},{18,... | collective-permute-start | bytes 430088 | tf_op jit(solution)/shard_map/ppermute | solution.py:31
  26.8 5.7 %collective-permute-start.7 = (bf16[560,128]{1,0:T(8,128)(2,1)S(1)}, bf16[560,128]{1,0:T(8,128)(2,1)S(1)}, u32[]{:S(2)}, u32[]{:S(2)}) collective-permute-start(bf16[560,128]{1,0:T(8,128)(2,1)S(1)} %get-tuple-element.32), channel_id=1, source_target_pairs={{0,4},{4,0},{2,6},{6,2},{8,12},{12,8},{10,14},{14,10},{16,20},{20,... | collective-permute-start | bytes 430088 | tf_op jit(solution)/shard_map/ppermute | solution.py:31
  31.2 5.8 %collective-permute-start.3 = (bf16[560,128]{1,0:T(8,128)(2,1)S(1)}, bf16[560,128]{1,0:T(8,128)(2,1)S(1)}, u32[]{:S(2)}, u32[]{:S(2)}) collective-permute-start(bf16[560,128]{1,0:T(8,128)(2,1)S(1)} %get-tuple-element.24), channel_id=1, source_target_pairs={{0,4},{4,0},{2,6},{6,2},{8,12},{12,8},{10,14},{14,10},{16,20},{20,... | collective-permute-start | bytes 430088 | tf_op jit(solution)/shard_map/ppermute | solution.py:31
  35.4 6.0 %collective-permute-start.8 = (bf16[560,128]{1,0:T(8,128)(2,1)S(1)}, bf16[560,128]{1,0:T(8,128)(2,1)S(1)}, u32[]{:S(2)}, u32[]{:S(2)}) collective-permute-start(bf16[560,128]{1,0:T(8,128)(2,1)S(1)} %get-tuple-element.34), channel_id=1, source_target_pairs={{0,8},{8,0},{2,10},{10,2},{4,12},{12,4},{6,14},{14,6},{16,24},{24,... | collective-permute-start | bytes 430088 | tf_op jit(solution)/shard_map/ppermute | solution.py:31
  40.1 6.8 %collective-permute-start.4 = (bf16[560,128]{1,0:T(8,128)(2,1)S(1)}, bf16[560,128]{1,0:T(8,128)(2,1)S(1)}, u32[]{:S(2)}, u32[]{:S(2)}) collective-permute-start(bf16[560,128]{1,0:T(8,128)(2,1)S(1)} %get-tuple-element.26), channel_id=1, source_target_pairs={{0,8},{8,0},{2,10},{10,2},{4,12},{12,4},{6,14},{14,6},{16,24},{24,... | collective-permute-start | bytes 430088 | tf_op jit(solution)/shard_map/ppermute | solution.py:31
  44.2 12.2 %collective-permute-start.9 = (bf16[560,128]{1,0:T(8,128)(2,1)S(1)}, bf16[560,128]{1,0:T(8,128)(2,1)S(1)}, u32[]{:S(2)}, u32[]{:S(2)}) collective-permute-start(bf16[560,128]{1,0:T(8,128)(2,1)S(1)} %get-tuple-element.36), channel_id=1, source_target_pairs={{0,16},{16,0},{2,18},{18,2},{4,20},{20,4},{6,22},{22,6},{8,24},{24... | collective-permute-start | bytes 430088 | tf_op jit(solution)/shard_map/ppermute | solution.py:31
  49.7 11.2 %collective-permute-start.5 = (bf16[560,128]{1,0:T(8,128)(2,1)S(1)}, bf16[560,128]{1,0:T(8,128)(2,1)S(1)}, u32[]{:S(2)}, u32[]{:S(2)}) collective-permute-start(bf16[560,128]{1,0:T(8,128)(2,1)S(1)} %get-tuple-element.28), channel_id=1, source_target_pairs={{0,16},{16,0},{2,18},{18,2},{4,20},{20,4},{6,22},{22,6},{8,24},{24... | collective-permute-start | bytes 430088 | tf_op jit(solution)/shard_map/ppermute | solution.py:31
